TPU v7x, 512 devices: a whole 4x4x16 slice. The times are simulated.
512 devices in a mesh: section: 2 (over core), seq: 64 (over z, y), mp: 4 (over x).
Axes of the slice: x: 4, y: 4, z: 16, core: 2. Of those that a mesh axis runs over, the one named last changes fastest.
Arguments:
- span_states: bfloat16 [8192, 4096], P('seq', ('section', 'mp')), may hold values from -6 to 6
- queries: bfloat16 [8192, 4096], P('seq', ('section', 'mp')), may hold values from -6 to 6
- slot_span: int32 [128], P('seq'), may hold values from 0 to 127, as said below
- neighbour_ids: int32 [128, 256], P('seq'), may hold values from 0 to 63999, as said below
- neighbour_count: int32 [128], P('seq'), may hold values from 1 to 2
- table: bfloat16 [64000, 896], P('seq'), may hold values from -6 to 6
- cond_weight: bfloat16 [4096, 896], P(('section', 'mp')), may hold values from -0.09375 to 0.09375
- kv_weight: bfloat16 [896, 2, 4096], P(None, None, ('section', 'mp')), may hold values from -0.1875 to 0.1875
Outputs:
- attended: bfloat16 [8192, 4096], P('seq', ('section', 'mp'))
Inputs may be any that keep to these rules, and one draw needn't show every extreme that they name: `slot_span`: A permutation of the 128 spans. The 2 slots of seq index i hold spans c with c // 2 equal to i - 1, i or i + 1 (cyclically over the seq indices), at most 1 from each side. `neighbour_ids`: over the spans of one seq index (c // 2 fixed), the ids at the 32 positions of one index g of section and mp (positions g * 32 to g * 32 + 31) fall at most 2 times into one block of 1000 consecutive ids, a bound that is reached; within one span at most once.
All inputs are finite; a program needn't handle non-finite values.
Results may differ from a plain program's by a relative error of at most 0.013.
Values may be sent and summed in bfloat16 or wider, within the bound.
A program may use at most 64 MiB of HBM per device.

v0:
```python
import math

import jax
import jax.numpy as jnp
from jax import lax
from jax.sharding import PartitionSpec as P

HD = 128
EHD = 128
NLEN = 128


def from_behind(array, axis, by):
    devices = lax.axis_size(axis)
    return lax.ppermute(array, axis, [(i, (i + by) % devices) for i in range(devices)])


def slot_positions(slot_span, seq_index, shards, count_spans):
    home_shard = slot_span // count_spans
    distance = jnp.mod(home_shard - seq_index, shards)
    side_pick = jnp.where(distance == 0, 1, jnp.where(distance == 1, 2, 0))
    return side_pick * count_spans + slot_span % count_spans


def lookup(ids, table, shards, capacity):
    flat_ids = ids.reshape(-1)
    vocab_rows = table.shape[0]
    owners = flat_ids // vocab_rows
    local_rows = flat_ids - owners * vocab_rows
    marks = (owners[:, None] == jnp.arange(shards, dtype=jnp.int32)[None, :]).astype(jnp.int32)
    rank_in = jnp.sum((jnp.cumsum(marks, axis=0) - 1) * marks, axis=1)
    target = owners * capacity + rank_in
    requests = (
        jnp.zeros((shards * capacity,), jnp.int32)
        .at[target]
        .set(local_rows)
        .reshape(shards, capacity)
    )
    table_rows = jnp.take(
        table, lax.all_to_all(requests, "seq", split_axis=0, concat_axis=0, tiled=True), axis=0
    )
    answers = lax.all_to_all(table_rows, "seq", split_axis=0, concat_axis=0, tiled=True)
    picked = jnp.take(answers.reshape(shards * capacity, table.shape[1]), target, axis=0)
    return picked.reshape(ids.shape + (table.shape[1],))


def encode(embedded, condition):
    count_spans, part_rows, enc_width = embedded.shape
    head_count = enc_width // EHD
    query_h = embedded.reshape(count_spans, part_rows, head_count, EHD)
    key_h = condition.reshape(count_spans, condition.shape[1], head_count, EHD)
    scores = jnp.einsum(
        "cphd,clhd->chpl", query_h, key_h, preferred_element_type=jnp.float32
    ) / math.sqrt(EHD)
    weights = jax.nn.softmax(scores, axis=-1).astype(jnp.bfloat16)
    attended_rows = jnp.einsum(
        "chpl,clhd->cphd", weights, key_h, preferred_element_type=jnp.float32
    )
    return (embedded.astype(jnp.float32) + attended_rows.reshape(embedded.shape)).astype(
        jnp.bfloat16
    )


def per_device(
    span_states, queries, slot_span, neighbour_ids, neighbour_count, table, cond_weight, kv_weight
):
    count_spans = slot_span.shape[0]
    enc_width = table.shape[1]
    shards = lax.axis_size("seq")
    seq_index = lax.axis_index("seq")
    groups = lax.axis_size("section") * lax.axis_size("mp")
    group_index = lax.axis_index("section") * lax.axis_size("mp") + lax.axis_index("mp")
    row_count = neighbour_ids.shape[1]
    part_rows = row_count // groups
    span_len = span_states.shape[0] // count_spans
    capacity = count_spans * ((part_rows + shards - 1) // shards)
    partial_value = jnp.dot(span_states, cond_weight, preferred_element_type=jnp.float32)
    condition = lax.psum(
        partial_value.reshape(count_spans, span_len, enc_width), ("section", "mp")
    ).astype(jnp.bfloat16)
    slot_index = slot_positions(slot_span, seq_index, shards, count_spans)
    side_parts = []
    for offset in (1, -1):
        side_parts.append(from_behind((condition, slot_span), "seq", offset))
    all_cond = jnp.concatenate([side_parts[0][0], condition, side_parts[1][0]], axis=0)
    all_slots = jnp.concatenate([side_parts[0][1], slot_span, side_parts[1][1]], axis=0)
    wanted = seq_index * count_spans + jnp.arange(count_spans, dtype=jnp.int32)
    matches = (all_slots[None, :] == wanted[:, None]).astype(jnp.int32)
    located = jnp.argmax(matches, axis=1)
    span_cond = jnp.take(all_cond, located, axis=0)
    own_ids = lax.dynamic_slice_in_dim(neighbour_ids, group_index * part_rows, part_rows, 1)
    span_encoded = encode(lookup(own_ids, table, shards, capacity), span_cond)
    returned = []
    for offset in (1, -1):
        returned.append(from_behind((span_encoded, neighbour_count), "seq", offset))
    all_rows = jnp.concatenate([returned[0][0], span_encoded, returned[1][0]], axis=0)
    all_counts = jnp.concatenate([returned[0][1], neighbour_count, returned[1][1]], axis=0)
    encoded = jnp.take(all_rows, slot_index, axis=0)
    counts = jnp.take(all_counts, slot_index, axis=0)
    key_value = jnp.einsum(
        "cre,ekf->crkf",
        lax.all_gather(encoded, ("section", "mp"), axis=1, tiled=True),
        kv_weight,
        preferred_element_type=jnp.float32,
    ).astype(jnp.bfloat16)
    local_heads = queries.shape[1] // HD
    query_h = queries.reshape(count_spans, span_len, local_heads, HD)
    key_h = key_value[:, :, 0].reshape(count_spans, row_count, local_heads, HD)
    value_h = key_value[:, :, 1].reshape(count_spans, row_count, local_heads, HD)
    scores = jnp.einsum(
        "clhd,crhd->chlr", query_h, key_h, preferred_element_type=jnp.float32
    ) / math.sqrt(HD)
    valid = jnp.arange(row_count, dtype=jnp.int32)[None, :] // NLEN < counts[:, None]
    scores = jnp.where(valid[:, None, None, :], scores, -jnp.inf)
    weights = jax.nn.softmax(scores, axis=-1).astype(jnp.bfloat16)
    output = jnp.einsum("chlr,crhd->clhd", weights, value_h, preferred_element_type=jnp.float32)
    return output.astype(jnp.bfloat16).reshape(queries.shape)


def solution(mesh):
    placed = (
        P("seq", ("section", "mp")),
        P("seq", ("section", "mp")),
        P("seq"),
        P("seq", None),
        P("seq"),
        P("seq", None),
        P(("section", "mp"), None),
        P(None, None, ("section", "mp")),
    )
    return jax.shard_map(
        per_device,
        mesh=mesh,
        in_specs=placed,
        out_specs=P("seq", ("section", "mp")),
        check_vma=False,
    )
```

profile of v0, /device:TPU:1, one launch (start us, length us, event | category | flops | bytes accessed | tf_op | source)
XLA Modules:
  0.0 161.5 jit_solution(18024520430283010897)
XLA Ops:
  0.0 1.7 %fusion.42 = f32[128,896]{1,0:T(8,128)S(1)} fusion(bf16[128,512]{1,0:T(8,128)(2,1)} %param.8, bf16[512,896]{1,0:T(8,128)(2,1)} %param.14), kind=kOutput, calls=%fused_computation.103 | convolution fusion | flops 117440512 | bytes 1507328 | tf_op jit(solution)/shard_map/dot_general | solution.py:77
  1.7 35.9 %all-reduce.1 = bf16[2,64,896]{2,1,0:T(8,128)(2,1)S(1)} all-reduce(f32[2,64,896]{2,1,0:T(8,128)S(1)} %bitcast.55), channel_id=1, replica_groups=mesh['section'=2,'seq'=64,'mp'=4] {'section','mp'}, use_global_device_ids=true, to_apply=%region_4.5 | all-reduce | flops 114688 | bytes 688128 | tf_op jit(solution)/shard_map/psum | solution.py:78
  37.7 1.9 %collective-permute-start.2 = (bf16[2,64,896]{2,1,0:T(8,128)(2,1)S(1)}, bf16[2,64,896]{2,1,0:T(8,128)(2,1)S(1)}, u32[]{:S(2)}, u32[]{:S(2)}) collective-permute-start(bf16[2,64,896]{2,1,0:T(8,128)(2,1)S(1)} %all-reduce.1), channel_id=1, source_target_pairs={{0,4},{4,8},{8,12},{12,16},{16,20},{20,24},{24,28},{28,32},{32,36}... | collective-permute-start | bytes 688136 | tf_op jit(solution)/shard_map/ppermute | solution.py:15
  39.6 11.6 %collective-permute-start.3 = (bf16[2,64,896]{2,1,0:T(8,128)(2,1)S(1)}, bf16[2,64,896]{2,1,0:T(8,128)(2,1)S(1)}, u32[]{:S(2)}, u32[]{:S(2)}) collective-permute-start(bf16[2,64,896]{2,1,0:T(8,128)(2,1)S(1)} %all-reduce.1), channel_id=1, source_target_pairs={{0,252},{4,0},{8,4},{12,8},{16,12},{20,16},{24,20},{28,24},{32,28}... | collective-permute-start | bytes 688136 | tf_op jit(solution)/shard_map/ppermute | solution.py:15
  51.3 1.9 %collective-permute-start = (s32[2]{0:T(128)S(1)}, s32[2]{0:T(128)S(1)}, u32[]{:S(2)}, u32[]{:S(2)}) collective-permute-start(s32[2]{0:T(128)S(1)} %copy-done.3), channel_id=1, source_target_pairs={{0,4},{4,8},{8,12},{12,16},{16,20},{20,24},{24,28},{28,32},{32,36}... | collective-permute-start | bytes 32 | tf_op jit(solution)/shard_map/ppermute | solution.py:15
  53.2 6.7 %collective-permute-start.1 = (s32[2]{0:T(128)S(1)}, s32[2]{0:T(128)S(1)}, u32[]{:S(2)}, u32[]{:S(2)}) collective-permute-start(s32[2]{0:T(128)S(1)} %copy-done.3), channel_id=1, source_target_pairs={{0,252},{4,0},{8,4},{12,8},{16,12},{20,16},{24,20},{28,24},{32,28}... | collective-permute-start | bytes 32 | tf_op jit(solution)/shard_map/ppermute | solution.py:15
  59.9 0.1 constant_dynamic-slice_fusion
  60.0 0.1 reshape.239
  60.1 0.1 fusion.25
  60.1 0.1 reduce_window_sum.11
  60.2 0.2 select_reduce_fusion
  60.4 0.1 reduce_sum.32
  60.5 0.1 compare_and_fusion.2
  60.6 0.1 and.90
  60.7 0.1 div.75
  60.8 0.8 scatter_custom_fusion
  61.6 0.8 all_to_all.13
  62.3 8.9 %all-to-all-start = ((s32[64,1,2]{2,1,0:T(1,128)}), s32[64,1,2]{2,1,0:T(1,128)S(1)}, u32[]{:S(2)}, u32[]{:S(2)}) async-start(s32[64,1,2]{2,1,0:T(1,128)} %bitcast.2), calls=%async_computation | async-start | bytes 65536 | tf_op jit(solution)/shard_map/all_to_all | solution.py:40
  71.3 2.9 %collective-permute-start.6 = (s32[2]{0:T(128)S(1)}, s32[2]{0:T(128)S(1)}, u32[]{:S(2)}, u32[]{:S(2)}) collective-permute-start(s32[2]{0:T(128)S(1)} %copy-done.5), channel_id=1, source_target_pairs={{0,4},{4,8},{8,12},{12,16},{16,20},{20,24},{24,28},{28,32},{32,36}... | collective-permute-start | bytes 32 | tf_op jit(solution)/shard_map/ppermute | solution.py:15
  74.3 5.7 %collective-permute-start.7 = (s32[2]{0:T(128)S(1)}, s32[2]{0:T(128)S(1)}, u32[]{:S(2)}, u32[]{:S(2)}) collective-permute-start(s32[2]{0:T(128)S(1)} %copy-done.5), channel_id=1, source_target_pairs={{0,252},{4,0},{8,4},{12,8},{16,12},{20,16},{24,20},{28,24},{32,28}... | collective-permute-start | bytes 32 | tf_op jit(solution)/shard_map/ppermute | solution.py:15
  80.0 0.1 pad_add_fusion.1
  80.1 0.8 fusion.28
  80.9 3.7 %all-to-all-done = s32[64,1,2]{2,1,0:T(1,128)S(1)} async-done(((s32[64,1,2]{2,1,0:T(1,128)}), s32[64,1,2]{2,1,0:T(1,128)S(1)}, u32[]{:S(2)}, u32[]{:S(2)}) %all-to-all-start) | async-done | bytes 544 | tf_op jit(solution)/shard_map/all_to_all | solution.py:40
  84.6 0.1 copy.46
  84.7 0.1 copy.49
  84.8 0.1 reshape.247
  85.0 0.9 gather_fusion
  85.9 0.1 reshape.246
  86.0 0.1 copy.47
  86.1 1.0 broadcast_select_fusion
  87.1 8.4 %all-to-all-start.1 = ((bf16[64,2,896]{2,1,0:T(2,128)(2,1)}), bf16[64,2,896]{2,1,0:T(2,128)(2,1)S(1)}, u32[]{:S(2)}, u32[]{:S(2)}) async-start(bf16[64,2,896]{2,1,0:T(2,128)(2,1)} %broadcast_select_fusion), calls=%async_computation.1 | async-start | bytes 458752 | tf_op jit(solution)/shard_map/all_to_all | solution.py:42
  95.5 0.5 compare_and_fusion
  96.0 0.1 pad_add_fusion
  96.1 0.6 gather_fusion.4
  96.7 0.5 broadcast_select_fusion.4
  97.2 0.1 pad_maximum_fusion
  97.3 0.6 gather_fusion.2
  97.9 0.3 gather.30
  98.2 0.8 broadcast_select_fusion.1
  99.0 13.4 %all-to-all-done.1 = bf16[64,2,896]{2,1,0:T(2,128)(2,1)S(1)} async-done(((bf16[64,2,896]{2,1,0:T(2,128)(2,1)}), bf16[64,2,896]{2,1,0:T(2,128)(2,1)S(1)}, u32[]{:S(2)}, u32[]{:S(2)}) %all-to-all-start.1) | async-done | bytes 229408 | tf_op jit(solution)/shard_map/all_to_all | solution.py:42
  112.4 0.1 reshape.240
  112.5 0.7 gather_fusion.1
  113.2 0.2 gather.31
  113.3 0.1 broadcast_select_fusion.2
  113.5 0.2 convolution_multiply_fusion.1
  113.7 0.2 fusion.40
  114.0 0.8 convolution_bitcast_fusion
  114.8 0.1 fusion.19
  114.9 3.1 %collective-permute-start.4 = (bf16[2,32,896]{2,1,0:T(8,128)(2,1)S(1)}, bf16[2,32,896]{2,1,0:T(8,128)(2,1)S(1)}, u32[]{:S(2)}, u32[]{:S(2)}) collective-permute-start(bf16[2,32,896]{2,1,0:T(8,128)(2,1)S(1)} %fusion.19), channel_id=1, source_target_pairs={{0,4},{4,8},{8,12},{12,16},{16,20},{20,24},{24,28},{28,32},{32,36}... | collective-permute-start | bytes 344072 | tf_op jit(solution)/shard_map/ppermute | solution.py:15
  118.0 5.5 %collective-permute-start.5 = (bf16[2,32,896]{2,1,0:T(8,128)(2,1)S(1)}, bf16[2,32,896]{2,1,0:T(8,128)(2,1)S(1)}, u32[]{:S(2)}, u32[]{:S(2)}) collective-permute-start(bf16[2,32,896]{2,1,0:T(8,128)(2,1)S(1)} %fusion.19), channel_id=1, source_target_pairs={{0,252},{4,0},{8,4},{12,8},{16,12},{20,16},{24,20},{28,24},{32,28}... | collective-permute-start | bytes 344072 | tf_op jit(solution)/shard_map/ppermute | solution.py:15
  123.5 0.1 broadcast_compare_fusion
  123.6 0.2 collective-permute-done.4
  123.7 1.5 collective-permute-done.5
  125.3 0.6 gather_fusion.3
  125.9 0.1 broadcast_select_fusion.3
  126.0 30.1 %all_gather.3 = bf16[2,256,896]{2,1,0:T(8,128)(2,1)S(1)} all-gather(bf16[2,32,896]{2,1,0:T(8,128)(2,1)S(1)} %broadcast_select_fusion.3), channel_id=1, replica_groups=mesh['section'=2,'seq'=64,'mp'=4] {'section','mp'}, dimensions={1}, use_global_device_ids=true | all-gather | bytes 1032192 | tf_op jit(solution)/shard_map/all_gather | solution.py:102
  156.1 2.7 %fusion.5 = bf16[2,256,2,512]{3,1,2,0:T(8,128)(2,1)S(1)} fusion(bf16[896,2,512]{2,1,0:T(2,128)(2,1)} %param.15, bf16[2,256,896]{2,1,0:T(8,128)(2,1)S(1)} %all_gather.3), kind=kOutput, calls=%fused_computation.11 | convolution fusion | flops 940048384 | bytes 3801088 | tf_op jit(solution)/shard_map/cre,ekf->crkf/dot_general | solution.py:100
  158.9 0.1 reshape_squeeze.7
  159.1 0.3 fusion.11
  159.4 0.3 fusion.41
  159.6 0.1 reshape_squeeze.6
  159.8 1.0 fusion.14
  160.7 0.1 copy.58
  160.8 0.7 copy.82
  (33 shorter events, 0.3 us)
Async XLA Ops:
  0.0 85.0 %copy-start = (bf16[1000,896]{1,0:T(8,128)(2,1)S(1)}, bf16[1000,896]{1,0:T(8,128)(2,1)}, u32[]{:S(2)}) copy-start(bf16[1000,896]{1,0:T(8,128)(2,1)} %param.13) | copy-start | bytes 5376004
  0.0 51.2 %copy-start.3 = (s32[2]{0:T(128)S(1)}, s32[2]{0:T(128)}, u32[]{:S(2)}) copy-start(s32[2]{0:T(128)} %param.10) | copy-start | bytes 28
  0.0 59.9 %copy-start.2 = (s32[2,256]{1,0:T(2,128)S(1)}, s32[2,256]{1,0:T(2,128)}, u32[]{:S(2)}) copy-start(s32[2,256]{1,0:T(2,128)} %param.11) | copy-start | bytes 6148
  0.0 71.3 %copy-start.5 = (s32[2]{0:T(128)S(1)}, s32[2]{0:T(128)}, u32[]{:S(2)}) copy-start(s32[2]{0:T(128)} %param.12) | copy-start | bytes 28
  0.0 74.3 %copy-start.1 = (bf16[128,512]{1,0:T(8,128)(2,1)S(1)}, bf16[128,512]{1,0:T(8,128)(2,1)}, u32[]{:S(2)}) copy-start(bf16[128,512]{1,0:T(8,128)(2,1)} %param.9) | copy-start | bytes 393220
  37.7 59.6 %collective-permute-start.2 = (bf16[2,64,896]{2,1,0:T(8,128)(2,1)S(1)}, bf16[2,64,896]{2,1,0:T(8,128)(2,1)S(1)}, u32[]{:S(2)}, u32[]{:S(2)}) collective-permute-start(bf16[2,64,896]{2,1,0:T(8,128)(2,1)S(1)} %all-reduce.1), channel_id=1, source_target_pairs={{0,4},{4,8},{8,12},{12,16},{16,20},{20,24},{24,28},{28,32},{32,36}... | collective-permute-start | bytes 688136 | tf_op jit(solution)/shard_map/ppermute | solution.py:15
  39.6 57.6 %collective-permute-start.3 = (bf16[2,64,896]{2,1,0:T(8,128)(2,1)S(1)}, bf16[2,64,896]{2,1,0:T(8,128)(2,1)S(1)}, u32[]{:S(2)}, u32[]{:S(2)}) collective-permute-start(bf16[2,64,896]{2,1,0:T(8,128)(2,1)S(1)} %all-reduce.1), channel_id=1, source_target_pairs={{0,252},{4,0},{8,4},{12,8},{16,12},{20,16},{24,20},{28,24},{32,28}... | collective-permute-start | bytes 688136 | tf_op jit(solution)/shard_map/ppermute | solution.py:15
  51.3 23.1 %collective-permute-start = (s32[2]{0:T(128)S(1)}, s32[2]{0:T(128)S(1)}, u32[]{:S(2)}, u32[]{:S(2)}) collective-permute-start(s32[2]{0:T(128)S(1)} %copy-done.3), channel_id=1, source_target_pairs={{0,4},{4,8},{8,12},{12,16},{16,20},{20,24},{24,28},{28,32},{32,36}... | collective-permute-start | bytes 32 | tf_op jit(solution)/shard_map/ppermute | solution.py:15
  53.2 26.9 %collective-permute-start.1 = (s32[2]{0:T(128)S(1)}, s32[2]{0:T(128)S(1)}, u32[]{:S(2)}, u32[]{:S(2)}) collective-permute-start(s32[2]{0:T(128)S(1)} %copy-done.3), channel_id=1, source_target_pairs={{0,252},{4,0},{8,4},{12,8},{16,12},{20,16},{24,20},{28,24},{32,28}... | collective-permute-start | bytes 32 | tf_op jit(solution)/shard_map/ppermute | solution.py:15
  62.3 22.3 %all-to-all-start = ((s32[64,1,2]{2,1,0:T(1,128)}), s32[64,1,2]{2,1,0:T(1,128)S(1)}, u32[]{:S(2)}, u32[]{:S(2)}) async-start(s32[64,1,2]{2,1,0:T(1,128)} %bitcast.2), calls=%async_computation | async-start | bytes 65536 | tf_op jit(solution)/shard_map/all_to_all | solution.py:40
  71.3 24.7 %collective-permute-start.6 = (s32[2]{0:T(128)S(1)}, s32[2]{0:T(128)S(1)}, u32[]{:S(2)}, u32[]{:S(2)}) collective-permute-start(s32[2]{0:T(128)S(1)} %copy-done.5), channel_id=1, source_target_pairs={{0,4},{4,8},{8,12},{12,16},{16,20},{20,24},{24,28},{28,32},{32,36}... | collective-permute-start | bytes 32 | tf_op jit(solution)/shard_map/ppermute | solution.py:15
  74.3 21.6 %collective-permute-start.7 = (s32[2]{0:T(128)S(1)}, s32[2]{0:T(128)S(1)}, u32[]{:S(2)}, u32[]{:S(2)}) collective-permute-start(s32[2]{0:T(128)S(1)} %copy-done.5), channel_id=1, source_target_pairs={{0,252},{4,0},{8,4},{12,8},{16,12},{20,16},{24,20},{28,24},{32,28}... | collective-permute-start | bytes 32 | tf_op jit(solution)/shard_map/ppermute | solution.py:15
  87.1 25.3 %all-to-all-start.1 = ((bf16[64,2,896]{2,1,0:T(2,128)(2,1)}), bf16[64,2,896]{2,1,0:T(2,128)(2,1)S(1)}, u32[]{:S(2)}, u32[]{:S(2)}) async-start(bf16[64,2,896]{2,1,0:T(2,128)(2,1)} %broadcast_select_fusion), calls=%async_computation.1 | async-start | bytes 458752 | tf_op jit(solution)/shard_map/all_to_all | solution.py:42
  112.5 11.1 %copy-start.4 = (s32[2]{0:T(128)S(1)}, s32[2]{0:T(128)}, u32[]{:S(2)}) copy-start(s32[2]{0:T(128)} %broadcast_select_fusion.4) | copy-start | bytes 28
  114.9 8.9 %collective-permute-start.4 = (bf16[2,32,896]{2,1,0:T(8,128)(2,1)S(1)}, bf16[2,32,896]{2,1,0:T(8,128)(2,1)S(1)}, u32[]{:S(2)}, u32[]{:S(2)}) collective-permute-start(bf16[2,32,896]{2,1,0:T(8,128)(2,1)S(1)} %fusion.19), channel_id=1, source_target_pairs={{0,4},{4,8},{8,12},{12,16},{16,20},{20,24},{24,28},{28,32},{32,36}... | collective-permute-start | bytes 344072 | tf_op jit(solution)/shard_map/ppermute | solution.py:15
  118.0 7.3 %collective-permute-start.5 = (bf16[2,32,896]{2,1,0:T(8,128)(2,1)S(1)}, bf16[2,32,896]{2,1,0:T(8,128)(2,1)S(1)}, u32[]{:S(2)}, u32[]{:S(2)}) collective-permute-start(bf16[2,32,896]{2,1,0:T(8,128)(2,1)S(1)} %fusion.19), channel_id=1, source_target_pairs={{0,252},{4,0},{8,4},{12,8},{16,12},{20,16},{24,20},{28,24},{32,28}... | collective-permute-start | bytes 344072 | tf_op jit(solution)/shard_map/ppermute | solution.py:15
where the time goes:
time: 162 us
  blocking collectives  66 us (41%)
  starting transfers between devices  56.7 us (35%)
  waiting for transfers between devices  18.8 us (12%)
  local copies, waits for them, and re-layouts  7.52 us (5%)
  matrix products  6.73 us (4%)
  other arithmetic  5.26 us (3%)
    ppermute x8, starting transfers between devices, from_behind(): lax.ppermute(array, axis, [(i, (i + by) % devices) for i in range(devices)])  39.4 us
    psum x1, blocking collectives, per_device(): lax.psum(partial_value.reshape(count_spans, span_len, enc_width), ('secti...  35.9 us
    all_gather x1, blocking collectives, per_device(): lax.all_gather(encoded, ('section', 'mp'), axis=1, tiled=True)  30.1 us
    all_to_all x1, waiting for transfers between devices, lookup(): lax.all_to_all(table_rows, 'seq', split_axis=0, concat_axis=0, tiled=True)  13.4 us
    all_to_all x1, starting transfers between devices, lookup(): lax.all_to_all(requests, 'seq', split_axis=0, concat_axis=0, tiled=True)  8.94 us
    all_to_all x1, starting transfers between devices, lookup(): lax.all_to_all(table_rows, 'seq', split_axis=0, concat_axis=0, tiled=True)  8.4 us
    all_to_all x1, waiting for transfers between devices, lookup(): lax.all_to_all(requests, 'seq', split_axis=0, concat_axis=0, tiled=True)  3.73 us
  transfers between devices with their start and end apart: 10, of which 4 were waited for; matrix products, arithmetic and copies ran while one was open for 5% of the time, Pallas kernels for 0%

commit v1 on v0

v1 whole, which is shorter than its diff:
```python
import functools
import math

import jax
import jax.numpy as jnp
from jax import lax
from jax.experimental import pallas as pl
from jax.experimental.pallas import tpu as pltpu
from jax.sharding import PartitionSpec as P

HD = 128
LANES = 128
TILE = 16
BF16 = jnp.bfloat16
F32 = jnp.float32
MESH = pl.DeviceIdType.MESH


def to_column(row, rows):
    shape = (rows, row.shape[1])
    here = lax.broadcasted_iota(jnp.int32, shape, 0) == lax.broadcasted_iota(jnp.int32, shape, 1)
    return jnp.sum(jnp.where(here, row, 0.0), axis=1, keepdims=True)


def lane_sum(mask, values):
    return jnp.sum(jnp.where(mask, values, 0.0), axis=1, keepdims=True)


def kernel(
    sizes,
    slot_span,
    counts,
    ids,
    states_hbm,
    queries_hbm,
    table_hbm,
    cond_weight_hbm,
    kv_hbm,
    out,
    states,
    queries,
    table,
    cond_weight,
    kv_raw,
    kv_weight,
    kv_f32,
    facts,
    asked_f32,
    answers,
    arrived,
    picks,
    partial,
    partial_out,
    partial_in,
    condition,
    encoded,
    local_sems,
    facts_sems,
    row_sems,
    part_sems,
    cond_sems,
    enc_send,
    enc_recv,
):
    shards, sections, mps, spans, part, span_len = sizes
    groups = sections * mps
    enc_width = table.shape[1]
    heads = enc_width // LANES
    vocab = table.shape[0]
    me = lax.axis_index("seq")
    section = lax.axis_index("section")
    mp = lax.axis_index("mp")
    group = section * mps + mp

    loads = [
        pltpu.make_async_copy(src, dst, local_sems.at[n])
        for n, (src, dst) in enumerate(
            (
                (states_hbm, states),
                (cond_weight_hbm, cond_weight),
                (table_hbm, table),
                (kv_hbm, kv_raw),
                (queries_hbm, queries),
            )
        )
    ]
    for load in loads:
        load.start()

    def seq_peer(d):
        return {"seq": lax.rem(me + d, shards)}

    def group_peer(ds, dx):
        return {"section": lax.rem(section + ds, sections), "mp": lax.rem(mp + dx, mps)}

    group_steps = [(ds, dx) for ds in range(sections) for dx in range(mps)][1:]

    barrier = pltpu.get_barrier_semaphore()

    def greet(d, carry):
        pl.semaphore_signal(barrier, inc=1, device_id=seq_peer(d), device_id_type=MESH)
        return carry

    lax.fori_loop(1, shards, greet, 0)
    for ds, dx in group_steps:
        pl.semaphore_signal(barrier, inc=1, device_id=group_peer(ds, dx), device_id_type=MESH)

    lane = lax.broadcasted_iota(jnp.int32, (1, LANES), 1)
    chunks = ids.shape[1] // LANES
    per_chunk = LANES // part
    all_ids = ids[...]
    own_ids = all_ids[:, :LANES]
    for c in range(1, chunks):
        own_ids = jnp.where(group // per_chunk == c, all_ids[:, c * LANES : (c + 1) * LANES], own_ids)
    own_ids = pltpu.roll(own_ids, lax.rem(LANES - lax.rem(group, per_chunk) * part, LANES), 1)
    message = jnp.zeros((1, LANES), jnp.int32)
    for k in range(spans):
        line = own_ids[k : k + 1]
        if k:
            line = pltpu.roll(line, k * part, 1)
        message = jnp.where((lane >= k * part) & (lane < (k + 1) * part), line, message)
        message = jnp.where(lane == spans * part + k, slot_span[k], message)
        message = jnp.where(lane == spans * part + spans + k, counts[k], message)
    facts[0:1, :] = message

    pl.semaphore_wait(barrier, shards - 1 + len(group_steps))

    def tell(d, carry):
        pltpu.make_async_remote_copy(
            src_ref=facts.at[pl.ds(0, 1)],
            dst_ref=facts.at[pl.ds(shards - d, 1)],
            send_sem=facts_sems.at[0],
            recv_sem=facts_sems.at[1],
            device_id=seq_peer(d),
            device_id_type=MESH,
        ).start()
        return carry

    lax.fori_loop(1, shards, tell, 0)

    loads[0].wait()
    loads[1].wait()
    product = jnp.dot(states[...], cond_weight[...], preferred_element_type=F32)
    block_rows = product.shape[0] // groups
    partial[...] = product.reshape(groups, block_rows, enc_width)
    partial_out[...] = product.astype(BF16).reshape(groups, block_rows, enc_width)
    for n, (ds, dx) in enumerate(group_steps):
        to = lax.rem(section + ds, sections) * mps + lax.rem(mp + dx, mps)
        back = ((sections - ds) % sections) * mps + (mps - dx) % mps
        pltpu.make_async_remote_copy(
            src_ref=partial_out.at[to],
            dst_ref=partial_in.at[back],
            send_sem=part_sems.at[0],
            recv_sem=part_sems.at[1],
            device_id=group_peer(ds, dx),
            device_id_type=MESH,
        ).start()

    loads[3].wait()
    pairs = kv_weight.shape[1] // LANES
    step_rows = kv_f32.shape[0] // pairs

    def split_pairs(step, carry):
        rows = pl.ds(pl.multiple_of(step * step_rows * pairs, TILE), step_rows * pairs)
        kv_f32[...] = kv_raw[rows, :].astype(F32)
        for t in range(pairs // 2):
            for j in range(2):
                column = (j * (pairs // 2) + t) * LANES
                kv_weight[pl.ds(pl.multiple_of(step * step_rows, TILE), step_rows), column : column + LANES] = (
                    kv_f32[pl.ds(t * 2 + j, step_rows, stride=pairs), :].astype(BF16)
                )
        return carry

    asked_f32[...] = jnp.zeros_like(asked_f32)

    def await_bytes(ref, sems):
        pltpu.make_async_remote_copy(
            src_ref=ref, dst_ref=ref, send_sem=sems.at[0], recv_sem=sems.at[1], device_id=seq_peer(1), device_id_type=MESH
        ).wait()

    await_bytes(facts.at[pl.ds(1, shards - 1)], facts_sems)

    told = facts[...]
    told_f32 = told.astype(F32)
    wide = told.shape
    lanes = lax.broadcasted_iota(jnp.int32, wide, 1)
    rows_d = lax.broadcasted_iota(jnp.int32, wide, 0)
    local = told - me * vocab
    inside = (local >= 0) & (local < vocab)
    local_f32 = (local + 1).astype(F32)
    want_row = jnp.zeros((1, LANES), F32)
    for k in range(spans):
        want = lane_sum(inside & (lanes >= k * part) & (lanes < (k + 1) * part), local_f32)
        want_row += jnp.sum(jnp.where(lanes == rows_d + k * shards, want, 0.0), axis=0, keepdims=True)
    span_row = (lax.rem(me + lax.rem(lane, shards), shards) * spans + lane // shards).astype(F32)
    span_row = jnp.where(lane < spans * shards, span_row, -1.0)
    loads[2].wait()
    marks = []
    vocab_lane = lax.broadcasted_iota(jnp.int32, (shards, vocab), 1).astype(F32)
    for k in range(spans):
        slot_holds = lane_sum(lanes == spans * part + k, told_f32)
        request = lane_sum(span_row == slot_holds, want_row) - 1.0
        marks.append((vocab_lane == request).astype(F32).astype(BF16))
    rows_out = jnp.dot(jnp.concatenate(marks, axis=0), table[...], preferred_element_type=F32)
    for k in range(spans):
        for h in range(heads):
            asked_f32[pl.ds(k * heads + h, shards, stride=TILE), :] = rows_out[
                k * shards : (k + 1) * shards, h * LANES : (h + 1) * LANES
            ]
    answers[...] = asked_f32[...].astype(BF16).reshape(answers.shape)

    def answer(d, carry):
        pltpu.make_async_remote_copy(
            src_ref=answers.at[d],
            dst_ref=arrived.at[shards - d],
            send_sem=row_sems.at[0],
            recv_sem=row_sems.at[1],
            device_id=seq_peer(d),
            device_id_type=MESH,
        ).start()
        return carry

    lax.fori_loop(1, shards, answer, 0)
    arrived[0] = answers[0]

    await_bytes(partial_in.at[pl.ds(1, groups - 1)], part_sems)
    total = partial[group]
    for n in range(1, groups):
        total += partial_in[n].astype(F32)
    condition[group] = total.astype(BF16)
    for ds, dx in group_steps:
        pltpu.make_async_remote_copy(
            src_ref=condition.at[group],
            dst_ref=condition.at[group],
            send_sem=cond_sems.at[0],
            recv_sem=cond_sems.at[1],
            device_id=group_peer(ds, dx),
            device_id_type=MESH,
        ).start()

    lax.fori_loop(0, kv_weight.shape[0] // step_rows, split_pairs, 0)

    kept = []
    place_lane = lax.broadcasted_iota(jnp.int32, (part, shards * TILE), 1).astype(F32)
    row_span = lax.rem(me + rows_d[:, :1], shards) * spans
    for k in range(spans):
        held = slot_span[k]
        id_row = jnp.zeros((1, LANES), F32)
        count = jnp.zeros((1, 1), F32)
        for home in range(spans):
            chosen = jnp.sum(jnp.where(row_span + home == held, told_f32, 0.0), axis=0, keepdims=True)
            moved = pltpu.roll(chosen, (LANES - home * part) % LANES, 1) if home else chosen
            id_row += moved
            count += lane_sum(lane == spans * part + spans + home, chosen)
        kept.append(count)
        owner = jnp.floor((id_row + 0.5) * (1.0 / vocab))
        step = owner - me.astype(F32)
        step = jnp.where(step < 0, step + shards, step)
        column = to_column(step * TILE, part)
        for h in range(heads):
            r = k * heads + h
            picks[r * part : (r + 1) * part, :] = (place_lane == column + r).astype(F32).astype(BF16)

    await_bytes(condition.at[pl.ds(0, groups - 1)], cond_sems)
    await_bytes(arrived.at[pl.ds(1, shards - 1)], row_sems)

    embedded = jnp.dot(
        picks[...], arrived[...].reshape(shards * TILE, LANES), preferred_element_type=F32
    )
    embedded_bf16 = embedded.astype(BF16)
    cond = condition[...].reshape(spans, span_len, enc_width)
    scores = []
    for k in range(spans):
        for h in range(heads):
            r = k * heads + h
            scores.append(
                lax.dot_general(
                    embedded_bf16[r * part : (r + 1) * part],
                    cond[k, :, h * LANES : (h + 1) * LANES],
                    (((1,), (1,)), ((), ())),
                    preferred_element_type=F32,
                )
            )
    weights = softmax(jnp.concatenate(scores, axis=0) * (1.0 / math.sqrt(LANES)))
    for k in range(spans):
        for h in range(heads):
            r = k * heads + h
            added = jnp.dot(
                weights[r * part : (r + 1) * part],
                cond[k, :, h * LANES : (h + 1) * LANES],
                preferred_element_type=F32,
            )
            encoded[group, k * part : (k + 1) * part, h * LANES : (h + 1) * LANES] = (
                embedded[r * part : (r + 1) * part] + added
            ).astype(BF16)

    def pass_on(index, block, target):
        return pltpu.make_async_remote_copy(
            src_ref=encoded.at[block],
            dst_ref=encoded.at[block],
            send_sem=enc_send.at[index],
            recv_sem=enc_recv.at[index],
            device_id=target,
            device_id_type=MESH,
        )

    sent = []
    for dx in range(1, mps):
        sent.append(pass_on(dx, group, group_peer(0, dx)))
        sent[-1].start()
    sibling = [pass_on(mps, group, group_peer(1, 0))]
    sibling[0].start()
    for dx in range(1, mps):
        block = section * mps + lax.rem(mp + mps - dx, mps)
        sent[dx - 1].wait_recv()
        onward = pass_on(mps + dx, block, group_peer(1, 0))
        onward.start()
        sibling.append(onward)
    for copy in sibling:
        copy.wait_recv()
    for copy in sent + sibling:
        copy.wait_send()

    loads[4].wait()
    rows = encoded[...].reshape(groups * spans * part, enc_width)
    key_value = jnp.dot(rows, kv_weight[...], preferred_element_type=F32).astype(BF16)
    width = kv_weight.shape[1] // 2
    local_heads = width // HD
    key_value = key_value.reshape(groups, spans, part, 2 * width)
    scores = []
    for k in range(spans):
        keys = key_value[:, k].reshape(groups * part, 2 * width)
        for t in range(local_heads):
            scores.append(
                lax.dot_general(
                    queries[k * span_len : (k + 1) * span_len, t * HD : (t + 1) * HD],
                    keys[:, t * HD : (t + 1) * HD],
                    (((1,), (1,)), ((), ())),
                    preferred_element_type=F32,
                )
            )
    neighbour = lax.broadcasted_iota(jnp.int32, scores[0].shape, 1) // (groups * part // sections)
    scores = [
        jnp.where(neighbour.astype(F32) < kept[n // local_heads], s * (1.0 / math.sqrt(HD)), -jnp.inf)
        for n, s in enumerate(scores)
    ]
    weights = softmax(jnp.concatenate(scores, axis=0))
    for k in range(spans):
        values = key_value[:, k].reshape(groups * part, 2 * width)
        for t in range(local_heads):
            n = k * local_heads + t
            out[k * span_len : (k + 1) * span_len, t * HD : (t + 1) * HD] = jnp.dot(
                weights[n * span_len : (n + 1) * span_len],
                values[:, width + t * HD : width + (t + 1) * HD],
                preferred_element_type=F32,
            ).astype(BF16)


def softmax(scores):
    high = jnp.max(scores, axis=1, keepdims=True)
    raised = jnp.exp(scores - high)
    return (raised / jnp.sum(raised, axis=1, keepdims=True)).astype(BF16)


def per_device(
    mesh_shape, span_states, queries, slot_span, neighbour_ids, neighbour_count, table, cond_weight, kv_weight
):
    shards, sections, mps = mesh_shape["seq"], mesh_shape["section"], mesh_shape["mp"]
    groups = sections * mps
    spans = slot_span.shape[0]
    part = neighbour_ids.shape[1] // groups
    tokens, width = queries.shape
    vocab, enc_width = table.shape
    pairs = 2 * width // LANES
    kv_rows = (
        kv_weight.reshape(enc_width, 2, width // LANES, LANES)
        .transpose(0, 2, 1, 3)
        .reshape(enc_width * pairs, LANES)
    )
    vmem = pl.BlockSpec(memory_space=pltpu.VMEM)
    smem = pl.BlockSpec(memory_space=pltpu.SMEM)
    hbm = pl.BlockSpec(memory_space=pl.ANY)
    rows_14 = spans * (enc_width // LANES)
    block_rows = tokens // groups
    dma = pltpu.SemaphoreType.DMA
    return pl.pallas_call(
        functools.partial(kernel, (shards, sections, mps, spans, part, tokens // spans)),
        out_shape=jax.ShapeDtypeStruct(queries.shape, queries.dtype),
        in_specs=[smem, smem, vmem, hbm, hbm, hbm, hbm, hbm],
        out_specs=vmem,
        scratch_shapes=[
            pltpu.VMEM(span_states.shape, BF16),
            pltpu.VMEM(queries.shape, BF16),
            pltpu.VMEM(table.shape, BF16),
            pltpu.VMEM(cond_weight.shape, BF16),
            pltpu.VMEM(kv_rows.shape, BF16),
            pltpu.VMEM((enc_width, 2 * width), BF16),
            pltpu.VMEM((enc_width // 8 * pairs, LANES), F32),
            pltpu.VMEM((shards, LANES), jnp.int32),
            pltpu.VMEM((shards * TILE, LANES), F32),
            pltpu.VMEM((shards, TILE, LANES), BF16),
            pltpu.VMEM((shards, TILE, LANES), BF16),
            pltpu.VMEM((rows_14 * part, shards * TILE), BF16),
            pltpu.VMEM((groups, block_rows, enc_width), F32),
            pltpu.VMEM((groups, block_rows, enc_width), BF16),
            pltpu.VMEM((groups, block_rows, enc_width), BF16),
            pltpu.VMEM((groups, block_rows, enc_width), BF16),
            pltpu.VMEM((groups, spans * part, enc_width), BF16),
            dma((5,)),
            dma((2,)),
            dma((2,)),
            dma((2,)),
            dma((2,)),
            dma((2 * mps,)),
            dma((2 * mps,)),
        ],
        compiler_params=pltpu.CompilerParams(
            collective_id=0, has_side_effects=True, vmem_limit_bytes=50 * 1024 * 1024
        ),
    )(slot_span, neighbour_count, neighbour_ids, span_states, queries, table, cond_weight, kv_rows)


def solution(mesh):
    placed = (
        P("seq", ("section", "mp")),
        P("seq", ("section", "mp")),
        P("seq"),
        P("seq", None),
        P("seq"),
        P("seq", None),
        P(("section", "mp"), None),
        P(None, None, ("section", "mp")),
    )
    return jax.shard_map(
        functools.partial(per_device, dict(mesh.shape)),
        mesh=mesh,
        in_specs=placed,
        out_specs=P("seq", ("section", "mp")),
        check_vma=False,
    )
```

time: 162 us -> 64.6 us (0.40)
  blocking collectives: 66 us -> 0 us
  Pallas kernels: 0 us -> 57.2 us
  starting transfers between devices: 56.7 us -> 0 us
  waiting for transfers between devices: 18.8 us -> 0 us
  matrix products: 6.73 us -> 0 us
  other arithmetic: 5.26 us -> 0 us
    pallas_call x0 -> x1, Pallas kernels: none -> 57.2 us  [per_device(): pl.pallas_call(functools.partial(kernel, (shards, sections, mps, spans, p...]
    ppermute x8 -> x0, starting transfers between devices: 39.4 us -> none  [from_behind(): lax.ppermute(array, axis, [(i, (i + by) % devices) for i in range(devices)])]
    psum x1 -> x0, blocking collectives: 35.9 us -> none  [per_device(): lax.psum(partial_value.reshape(count_spans, span_len, enc_width), ('secti...]
    all_gather x1 -> x0, blocking collectives: 30.1 us -> none  [per_device(): lax.all_gather(encoded, ('section', 'mp'), axis=1, tiled=True)]
    all_to_all x2 -> x0, starting transfers between devices: 17.3 us -> none  [the longest x1 8.94 us: lookup(): lax.all_to_all(requests, 'seq', split_axis=0, concat_axis=0, tiled=True)]
    all_to_all x2 -> x0, waiting for transfers between devices: 17.1 us -> none  [the longest x1 13.4 us: lookup(): lax.all_to_all(table_rows, 'seq', split_axis=0, concat_axis=0, tiled=True)]
    dot_general x6 -> x0, matrix products: 6.73 us -> none  [the longest x1 2.75 us: per_device(): jnp.einsum('cre,ekf->crkf', lax.all_gather(encoded, ('section', 'mp'), ax...]
    unnamed x13 -> x15, local copies, waits for them, and re-layouts: 0.7 us -> 7.12 us
  transfers between devices with their start and end apart: 10 -> 0, of which waited for: 4 -> 0; matrix products, arithmetic and copies ran while one was open for 5% -> 0% of each run, Pallas kernels for 0% -> 0%
where the time goes in v1:
time: 64.6 us; the launch traced here: 64.3 us
  Pallas kernels  57.2 us (89%)
  local copies, waits for them, and re-layouts  7.12 us (11%)
    pallas_call x1, Pallas kernels, per_device(): pl.pallas_call(functools.partial(kernel, (shards, sections, mps, spans, p...  57.2 us
    unnamed x15, local copies, waits for them, and re-layouts  7.12 us

profile of v1, /device:TPU:1, one launch (start us, length us, event | category | flops | bytes accessed | tf_op | source)
XLA Modules:
  0.0 64.3 jit_solution(15624744312584860940)
XLA Ops:
  0.0 0.0 copy-start
  0.0 1.5 %copy-done = bf16[1000,896]{1,0:T(8,128)(2,1)S(1)} copy-done((bf16[1000,896]{1,0:T(8,128)(2,1)S(1)}, bf16[1000,896]{1,0:T(8,128)(2,1)}, u32[]{:S(2)}) %copy-start) | copy-done | bytes 1792024
  1.5 0.0 copy-start.1
  1.5 1.2 %copy-done.1 = bf16[512,896]{1,0:T(8,128)(2,1)S(1)} copy-done((bf16[512,896]{1,0:T(8,128)(2,1)S(1)}, bf16[512,896]{1,0:T(8,128)(2,1)}, u32[]{:S(2)}) %copy-start.1) | copy-done | bytes 917528
  2.7 0.0 copy-start.2
  2.7 0.9 %copy-done.2 = bf16[128,512]{1,0:T(8,128)(2,1)S(1)} copy-done((bf16[128,512]{1,0:T(8,128)(2,1)S(1)}, bf16[128,512]{1,0:T(8,128)(2,1)}, u32[]{:S(2)}) %copy-start.2) | copy-done | bytes 131096
  3.6 0.0 copy-start.3
  3.6 0.9 %copy-done.3 = bf16[128,512]{1,0:T(8,128)(2,1)S(1)} copy-done((bf16[128,512]{1,0:T(8,128)(2,1)S(1)}, bf16[128,512]{1,0:T(8,128)(2,1)}, u32[]{:S(2)}) %copy-start.3) | copy-done | bytes 131096
  4.5 0.0 copy-start.4
  4.5 0.7 %copy-done.4 = s32[2,256]{1,0:T(2,128)S(1)} copy-done((s32[2,256]{1,0:T(2,128)S(1)}, s32[2,256]{1,0:T(2,128)}, u32[]{:S(2)}) %copy-start.4) | copy-done | bytes 2072
  5.2 0.0 copy-start.5
  5.2 0.7 %copy-done.5 = s32[2]{0:T(128)S(1)} copy-done((s32[2]{0:T(128)S(1)}, s32[2]{0:T(128)}, u32[]{:S(2)}) %copy-start.5) | copy-done | bytes 32
  5.8 0.0 copy-start.6
  5.8 0.7 %copy-done.6 = s32[2]{0:T(128)S(1)} copy-done((s32[2]{0:T(128)S(1)}, s32[2]{0:T(128)}, u32[]{:S(2)}) %copy-start.6) | copy-done | bytes 32
  6.5 57.2 %shard_map.82 = bf16[128,512]{1,0:T(8,128)(2,1)S(1)} custom-call(s32[2]{0:T(128)S(1)} %copy-done.5, s32[2]{0:T(128)S(1)} %copy-done.6, s32[2,256]{1,0:T(2,128)S(1)} %copy-done.4, bf16[128,512]{1,0:T(8,128)(2,1)S(1)} %copy-done.2, bf16[128,512]{1,0:T(8,128)(2,1)S(1)} %copy-done.3, bf16[1000,896]{1,0:T(8,128)(2,1)S(1)} %copy-done, ...), custom_call_target="tpu_custom_call" | custom-call | tf_op jit(solution)/shard_map/pallas_call | solution.py:386
  63.7 0.7 %copy.11 = bf16[128,512]{1,0:T(8,128)(2,1)} copy(bf16[128,512]{1,0:T(8,128)(2,1)S(1)} %shard_map.82) | data formatting | bytes 262144
Async XLA Ops:
  0.0 1.5 %copy-start = (bf16[1000,896]{1,0:T(8,128)(2,1)S(1)}, bf16[1000,896]{1,0:T(8,128)(2,1)}, u32[]{:S(2)}) copy-start(bf16[1000,896]{1,0:T(8,128)(2,1)} %table_hbm.1) | copy-start | bytes 5376004
  1.5 1.2 %copy-start.1 = (bf16[512,896]{1,0:T(8,128)(2,1)S(1)}, bf16[512,896]{1,0:T(8,128)(2,1)}, u32[]{:S(2)}) copy-start(bf16[512,896]{1,0:T(8,128)(2,1)} %cond_weight_hbm.1) | copy-start | bytes 2752516
  2.7 0.9 %copy-start.2 = (bf16[128,512]{1,0:T(8,128)(2,1)S(1)}, bf16[128,512]{1,0:T(8,128)(2,1)}, u32[]{:S(2)}) copy-start(bf16[128,512]{1,0:T(8,128)(2,1)} %states_hbm.1) | copy-start | bytes 393220
  3.6 0.9 %copy-start.3 = (bf16[128,512]{1,0:T(8,128)(2,1)S(1)}, bf16[128,512]{1,0:T(8,128)(2,1)}, u32[]{:S(2)}) copy-start(bf16[128,512]{1,0:T(8,128)(2,1)} %queries_hbm.1) | copy-start | bytes 393220
  4.5 0.7 %copy-start.4 = (s32[2,256]{1,0:T(2,128)S(1)}, s32[2,256]{1,0:T(2,128)}, u32[]{:S(2)}) copy-start(s32[2,256]{1,0:T(2,128)} %ids.1) | copy-start | bytes 6148
  5.2 0.7 %copy-start.5 = (s32[2]{0:T(128)S(1)}, s32[2]{0:T(128)}, u32[]{:S(2)}) copy-start(s32[2]{0:T(128)} %slot_span.1) | copy-start | bytes 28
  5.8 0.7 %copy-start.6 = (s32[2]{0:T(128)S(1)}, s32[2]{0:T(128)}, u32[]{:S(2)}) copy-start(s32[2]{0:T(128)} %counts.1) | copy-start | bytes 28

commit v2 on v1

v2 whole, which is shorter than its diff:
```python
import functools
import math

import jax
import jax.numpy as jnp
from jax import lax
from jax.experimental import pallas as pl
from jax.experimental.pallas import tpu as pltpu
from jax.sharding import PartitionSpec as P

HD = 128
LANES = 128
TILE = 16
BF16 = jnp.bfloat16
F32 = jnp.float32
MESH = pl.DeviceIdType.MESH


def to_column(row, rows):
    shape = (rows, row.shape[1])
    here = lax.broadcasted_iota(jnp.int32, shape, 0) == lax.broadcasted_iota(jnp.int32, shape, 1)
    return jnp.sum(jnp.where(here, row, 0.0), axis=1, keepdims=True)


def lane_sum(mask, values):
    return jnp.sum(jnp.where(mask, values, 0.0), axis=1, keepdims=True)


def kernel(
    sizes,
    slot_span_hbm,
    counts_hbm,
    ids_hbm,
    states_hbm,
    queries_hbm,
    table_hbm,
    cond_weight_hbm,
    kv_hbm,
    out,
    slot_span,
    counts,
    ids,
    states,
    queries,
    table,
    cond_weight,
    kv_raw,
    kv_weight,
    kv_f32,
    facts_near,
    facts_far,
    asked_f32,
    answers_near,
    answers_far,
    arrived,
    picks,
    partial,
    partial_out,
    partial_in,
    condition,
    encoded,
    local_sems,
    facts_sems,
    row_sems,
    part_sems,
    cond_sems,
    enc_send,
    enc_recv,
):
    shards, sections, mps, spans, part, span_len = sizes
    groups = sections * mps
    enc_width = table.shape[1]
    heads = enc_width // LANES
    vocab = table.shape[0]
    me = lax.axis_index("seq")
    section = lax.axis_index("section")
    mp = lax.axis_index("mp")
    group = section * mps + mp

    loads = [
        pltpu.make_async_copy(src, dst, local_sems.at[n])
        for n, (src, dst) in enumerate(
            (
                (states_hbm, states),
                (cond_weight_hbm, cond_weight),
                (table_hbm, table),
                (kv_hbm, kv_raw),
                (queries_hbm, queries),
                (ids_hbm, ids),
                (slot_span_hbm, slot_span),
                (counts_hbm, counts),
            )
        )
    ]
    for load in loads[5:] + loads[:5]:
        load.start()

    half, margin = shards // 2, shards // 4

    def seq_peer(d):
        return {"seq": lax.rem(me + d, shards)}

    def over_peers(low, high, act):
        def body(i, carry):
            act(half + (i + 1) // 2 * (1 - 2 * lax.rem(i, 2)))
            return carry

        lax.fori_loop(low, high, body, 0)

    def wait_in(ref, sem):
        pltpu.make_async_remote_copy(
            src_ref=ref, dst_ref=ref, send_sem=sem, recv_sem=sem, device_id=seq_peer(1), device_id_type=MESH
        ).wait_recv()

    def wait_out(ref, sem):
        pltpu.make_async_remote_copy(
            src_ref=ref, dst_ref=ref, send_sem=sem, recv_sem=sem, device_id=seq_peer(1), device_id_type=MESH
        ).wait_send()

    def group_peer(ds, dx):
        return {"section": lax.rem(section + ds, sections), "mp": lax.rem(mp + dx, mps)}

    group_steps = [(ds, dx) for ds in range(sections) for dx in range(mps)][1:]

    barrier = pltpu.get_barrier_semaphore()

    facts_near[...] = jnp.full(facts_near.shape, -1, jnp.int32)
    facts_far[...] = jnp.full(facts_far.shape, -1, jnp.int32)
    over_peers(
        0, shards - 1, lambda d: pl.semaphore_signal(barrier, inc=1, device_id=seq_peer(d), device_id_type=MESH)
    )
    for ds, dx in group_steps:
        pl.semaphore_signal(barrier, inc=1, device_id=group_peer(ds, dx), device_id_type=MESH)

    lane = lax.broadcasted_iota(jnp.int32, (1, LANES), 1)
    chunks = ids.shape[1] // LANES
    per_chunk = LANES // part
    for load in loads[5:]:
        load.wait()
    all_ids = ids[...]
    own_ids = all_ids[:, :LANES]
    for c in range(1, chunks):
        own_ids = jnp.where(group // per_chunk == c, all_ids[:, c * LANES : (c + 1) * LANES], own_ids)
    own_ids = pltpu.roll(own_ids, lax.rem(LANES - lax.rem(group, per_chunk) * part, LANES), 1)
    message = jnp.zeros((1, LANES), jnp.int32)
    for k in range(spans):
        line = own_ids[k : k + 1]
        if k:
            line = pltpu.roll(line, k * part, 1)
        message = jnp.where((lane >= k * part) & (lane < (k + 1) * part), line, message)
        message = jnp.where(lane == spans * part + k, slot_span[k], message)
        message = jnp.where(lane == spans * part + spans + k, counts[k], message)
    facts_near[0:1, :] = message

    pl.semaphore_wait(barrier, shards - 1 + len(group_steps))

    def tell(into, sem):
        def act(d):
            pltpu.make_async_remote_copy(
                src_ref=facts_near.at[pl.ds(0, 1)],
                dst_ref=into.at[pl.ds(shards - d, 1)],
                send_sem=facts_sems.at[0],
                recv_sem=sem,
                device_id=seq_peer(d),
                device_id_type=MESH,
            ).start()

        return act

    far_facts, far_rows = 2 * margin - 1, 2 * margin + 1
    over_peers(0, far_facts, tell(facts_far, facts_sems.at[1]))
    over_peers(far_facts, shards - 1, tell(facts_near, facts_sems.at[2]))

    loads[0].wait()
    loads[1].wait()
    product = jnp.dot(states[...], cond_weight[...], preferred_element_type=F32)
    block_rows = product.shape[0] // groups
    partial[...] = product.reshape(groups, block_rows, enc_width)
    partial_out[...] = product.astype(BF16).reshape(groups, block_rows, enc_width)
    for n, (ds, dx) in enumerate(group_steps):
        to = lax.rem(section + ds, sections) * mps + lax.rem(mp + dx, mps)
        back = ((sections - ds) % sections) * mps + (mps - dx) % mps
        pltpu.make_async_remote_copy(
            src_ref=partial_out.at[to],
            dst_ref=partial_in.at[back],
            send_sem=part_sems.at[0],
            recv_sem=part_sems.at[1],
            device_id=group_peer(ds, dx),
            device_id_type=MESH,
        ).start()

    loads[3].wait()
    pairs = kv_weight.shape[1] // LANES
    step_rows = kv_f32.shape[0] // pairs

    def split_pairs(step, carry):
        rows = pl.ds(pl.multiple_of(step * step_rows * pairs, TILE), step_rows * pairs)
        kv_f32[...] = kv_raw[rows, :].astype(F32)
        for t in range(pairs // 2):
            for j in range(2):
                column = (j * (pairs // 2) + t) * LANES
                kv_weight[pl.ds(pl.multiple_of(step * step_rows, TILE), step_rows), column : column + LANES] = (
                    kv_f32[pl.ds(t * 2 + j, step_rows, stride=pairs), :].astype(BF16)
                )
        return carry

    asked_f32[...] = jnp.zeros_like(asked_f32)

    wide = facts_near.shape
    lanes = lax.broadcasted_iota(jnp.int32, wide, 1)
    rows_d = lax.broadcasted_iota(jnp.int32, wide, 0)
    span_row = (lax.rem(me + lax.rem(lane, shards), shards) * spans + lane // shards).astype(F32)
    span_row = jnp.where(lane < spans * shards, span_row, -2.0)
    vocab_lane = lax.broadcasted_iota(jnp.int32, (shards, vocab), 1).astype(F32)

    def look_up(told, answers):
        told_f32 = told.astype(F32)
        local = told - me * vocab
        inside = (local >= 0) & (local < vocab)
        local_f32 = (local + 1).astype(F32)
        want_row = jnp.zeros((1, LANES), F32)
        for k in range(spans):
            want = lane_sum(inside & (lanes >= k * part) & (lanes < (k + 1) * part), local_f32)
            want_row += jnp.sum(jnp.where(lanes == rows_d + k * shards, want, 0.0), axis=0, keepdims=True)
        marks = []
        for k in range(spans):
            slot_holds = lane_sum(lanes == spans * part + k, told_f32)
            request = lane_sum(span_row == slot_holds, want_row) - 1.0
            marks.append((vocab_lane == request).astype(F32).astype(BF16))
        rows_out = jnp.dot(jnp.concatenate(marks, axis=0), table[...], preferred_element_type=F32)
        for k in range(spans):
            for h in range(heads):
                asked_f32[pl.ds(k * heads + h, shards, stride=TILE), :] = rows_out[
                    k * shards : (k + 1) * shards, h * LANES : (h + 1) * LANES
                ]
        answers[...] = asked_f32[...].astype(BF16).reshape(answers.shape)

    def answer(answers):
        def act(d):
            pltpu.make_async_remote_copy(
                src_ref=answers.at[d],
                dst_ref=arrived.at[shards - d],
                send_sem=row_sems.at[0],
                recv_sem=row_sems.at[1],
                device_id=seq_peer(d),
                device_id_type=MESH,
            ).start()

        return act

    loads[2].wait()
    wait_in(facts_near.at[pl.ds(0, shards - 1 - far_facts)], facts_sems.at[2])
    near = facts_near[...]
    look_up(near, answers_near)
    over_peers(far_rows, shards - 1, answer(answers_near))
    arrived[0] = answers_near[0]
    wait_in(facts_far.at[pl.ds(0, far_facts)], facts_sems.at[1])
    look_up(jnp.where((rows_d > half - margin) & (rows_d < half + margin), facts_far[...], near), answers_far)
    over_peers(0, far_rows, answer(answers_far))
    told_f32 = near.astype(F32)

    wait_in(partial_in.at[pl.ds(1, groups - 1)], part_sems.at[1])
    total = partial[group]
    for n in range(1, groups):
        total += partial_in[n].astype(F32)
    condition[group] = total.astype(BF16)
    for ds, dx in group_steps:
        pltpu.make_async_remote_copy(
            src_ref=condition.at[group],
            dst_ref=condition.at[group],
            send_sem=cond_sems.at[0],
            recv_sem=cond_sems.at[1],
            device_id=group_peer(ds, dx),
            device_id_type=MESH,
        ).start()

    lax.fori_loop(0, kv_weight.shape[0] // step_rows, split_pairs, 0)

    kept = []
    place_lane = lax.broadcasted_iota(jnp.int32, (part, shards * TILE), 1).astype(F32)
    row_span = lax.rem(me + rows_d[:, :1], shards) * spans
    for k in range(spans):
        held = slot_span[k]
        id_row = jnp.zeros((1, LANES), F32)
        count = jnp.zeros((1, 1), F32)
        for home in range(spans):
            chosen = jnp.sum(jnp.where(row_span + home == held, told_f32, 0.0), axis=0, keepdims=True)
            moved = pltpu.roll(chosen, (LANES - home * part) % LANES, 1) if home else chosen
            id_row += moved
            count += lane_sum(lane == spans * part + spans + home, chosen)
        kept.append(count)
        owner = jnp.floor((id_row + 0.5) * (1.0 / vocab))
        step = owner - me.astype(F32)
        step = jnp.where(step < 0, step + shards, step)
        column = to_column(step * TILE, part)
        for h in range(heads):
            r = k * heads + h
            picks[r * part : (r + 1) * part, :] = (place_lane == column + r).astype(F32).astype(BF16)

    wait_in(condition.at[pl.ds(0, groups - 1)], cond_sems.at[1])
    wait_in(arrived.at[pl.ds(1, shards - 1)], row_sems.at[1])

    def pass_on(k, index, block, target):
        copy = pltpu.make_async_remote_copy(
            src_ref=encoded.at[k, block],
            dst_ref=encoded.at[k, block],
            send_sem=enc_send.at[k, index],
            recv_sem=enc_recv.at[k, index],
            device_id=target,
            device_id_type=MESH,
        )
        copy.start()
        return copy

    over_x, to_sibling = [], []
    cond = condition[...].reshape(spans, span_len, enc_width)
    rows_in = arrived[...].reshape(shards * TILE, LANES)
    for k in range(spans):
        embedded = jnp.dot(
            picks[k * heads * part : (k + 1) * heads * part, :], rows_in, preferred_element_type=F32
        )
        embedded_bf16 = embedded.astype(BF16)
        scores = []
        for h in range(heads):
            scores.append(
                lax.dot_general(
                    embedded_bf16[h * part : (h + 1) * part],
                    cond[k, :, h * LANES : (h + 1) * LANES],
                    (((1,), (1,)), ((), ())),
                    preferred_element_type=F32,
                )
            )
        weights = softmax(jnp.concatenate(scores, axis=0) * (1.0 / math.sqrt(LANES)))
        for h in range(heads):
            added = jnp.dot(
                weights[h * part : (h + 1) * part],
                cond[k, :, h * LANES : (h + 1) * LANES],
                preferred_element_type=F32,
            )
            encoded[k, group, :, h * LANES : (h + 1) * LANES] = (
                embedded[h * part : (h + 1) * part] + added
            ).astype(BF16)
        over_x.append([pass_on(k, dx, group, group_peer(0, dx)) for dx in range(1, mps)])
        to_sibling.append([pass_on(k, mps, group, group_peer(1, 0))])

    def forward(k):
        for dx in range(1, mps):
            over_x[k][dx - 1].wait_recv()
            block = section * mps + lax.rem(mp + mps - dx, mps)
            to_sibling[k].append(pass_on(k, mps + dx, block, group_peer(1, 0)))

    def gathered(k):
        for copy in to_sibling[k]:
            copy.wait_recv()

    width = kv_weight.shape[1] // 2
    local_heads = width // HD
    row_count = groups * part

    def project(k):
        rows = encoded[k].reshape(row_count, enc_width)
        return jnp.dot(rows, kv_weight[...], preferred_element_type=F32).astype(BF16)

    def attend(k, key_value):
        scores = []
        for t in range(local_heads):
            scores.append(
                lax.dot_general(
                    queries[k * span_len : (k + 1) * span_len, t * HD : (t + 1) * HD],
                    key_value[:, t * HD : (t + 1) * HD],
                    (((1,), (1,)), ((), ())),
                    preferred_element_type=F32,
                )
            )
        scores = jnp.concatenate(scores, axis=0) * (1.0 / math.sqrt(HD))
        neighbour = lax.broadcasted_iota(jnp.int32, scores.shape, 1) // (row_count // sections)
        weights = softmax(jnp.where(neighbour.astype(F32) < kept[k], scores, -jnp.inf))
        for t in range(local_heads):
            out[k * span_len : (k + 1) * span_len, t * HD : (t + 1) * HD] = jnp.dot(
                weights[t * span_len : (t + 1) * span_len],
                key_value[:, width + t * HD : width + (t + 1) * HD],
                preferred_element_type=F32,
            ).astype(BF16)

    loads[4].wait()
    forward(0)
    gathered(0)
    for k in range(spans):
        key_value = project(k)
        if k + 1 < spans:
            forward(k + 1)
        attend(k, key_value)
        if k + 1 < spans:
            gathered(k + 1)

    wait_out(facts_far.at[pl.ds(0, shards - 1)], facts_sems.at[0])
    wait_out(answers_far.at[pl.ds(1, shards - 1)], row_sems.at[0])
    wait_out(partial_out.at[pl.ds(1, groups - 1)], part_sems.at[0])
    wait_out(condition.at[pl.ds(1, groups - 1)], cond_sems.at[0])
    for copy in sum(over_x + to_sibling, []):
        copy.wait_send()


def softmax(scores):
    high = jnp.max(scores, axis=1, keepdims=True)
    raised = jnp.exp(scores - high)
    return (raised / jnp.sum(raised, axis=1, keepdims=True)).astype(BF16)


def per_device(
    mesh_shape, span_states, queries, slot_span, neighbour_ids, neighbour_count, table, cond_weight, kv_weight
):
    shards, sections, mps = mesh_shape["seq"], mesh_shape["section"], mesh_shape["mp"]
    groups = sections * mps
    spans = slot_span.shape[0]
    part = neighbour_ids.shape[1] // groups
    tokens, width = queries.shape
    vocab, enc_width = table.shape
    pairs = 2 * width // LANES
    kv_rows = (
        kv_weight.reshape(enc_width, 2, width // LANES, LANES)
        .transpose(0, 2, 1, 3)
        .reshape(enc_width * pairs, LANES)
    )
    vmem = pl.BlockSpec(memory_space=pltpu.VMEM)
    hbm = pl.BlockSpec(memory_space=pltpu.HBM)
    rows_14 = spans * (enc_width // LANES)
    block_rows = tokens // groups
    dma = pltpu.SemaphoreType.DMA
    return pl.pallas_call(
        functools.partial(kernel, (shards, sections, mps, spans, part, tokens // spans)),
        out_shape=jax.ShapeDtypeStruct(queries.shape, queries.dtype),
        in_specs=[hbm] * 8,
        out_specs=vmem,
        scratch_shapes=[
            pltpu.SMEM(slot_span.shape, jnp.int32),
            pltpu.SMEM(neighbour_count.shape, jnp.int32),
            pltpu.VMEM(neighbour_ids.shape, jnp.int32),
            pltpu.VMEM(span_states.shape, BF16),
            pltpu.VMEM(queries.shape, BF16),
            pltpu.VMEM(table.shape, BF16),
            pltpu.VMEM(cond_weight.shape, BF16),
            pltpu.VMEM(kv_rows.shape, BF16),
            pltpu.VMEM((enc_width, 2 * width), BF16),
            pltpu.VMEM((enc_width // 8 * pairs, LANES), F32),
            pltpu.VMEM((shards, LANES), jnp.int32),
            pltpu.VMEM((shards, LANES), jnp.int32),
            pltpu.VMEM((shards * TILE, LANES), F32),
            pltpu.VMEM((shards, TILE, LANES), BF16),
            pltpu.VMEM((shards, TILE, LANES), BF16),
            pltpu.VMEM((shards, TILE, LANES), BF16),
            pltpu.VMEM((rows_14 * part, shards * TILE), BF16),
            pltpu.VMEM((groups, block_rows, enc_width), F32),
            pltpu.VMEM((groups, block_rows, enc_width), BF16),
            pltpu.VMEM((groups, block_rows, enc_width), BF16),
            pltpu.VMEM((groups, block_rows, enc_width), BF16),
            pltpu.VMEM((spans, groups, part, enc_width), BF16),
            dma((8,)),
            dma((3,)),
            dma((2,)),
            dma((2,)),
            dma((2,)),
            dma((spans, 2 * mps)),
            dma((spans, 2 * mps)),
        ],
        compiler_params=pltpu.CompilerParams(
            collective_id=0, has_side_effects=True, vmem_limit_bytes=60 * 1024 * 1024
        ),
    )(slot_span, neighbour_count, neighbour_ids, span_states, queries, table, cond_weight, kv_rows)


def solution(mesh):
    placed = (
        P("seq", ("section", "mp")),
        P("seq", ("section", "mp")),
        P("seq"),
        P("seq", None),
        P("seq"),
        P("seq", None),
        P(("section", "mp"), None),
        P(None, None, ("section", "mp")),
    )
    return jax.shard_map(
        functools.partial(per_device, dict(mesh.shape)),
        mesh=mesh,
        in_specs=placed,
        out_specs=P("seq", ("section", "mp")),
        check_vma=False,
    )
```

time: 64.6 us -> 53.4 us (0.83)
  local copies, waits for them, and re-layouts: 7.12 us -> 1.57 us
  Pallas kernels: 57.2 us -> 51.7 us
    unnamed x15 -> x1, local copies, waits for them, and re-layouts: 7.12 us -> 1.57 us
    pallas_call x1, Pallas kernels: 57.2 us -> 51.7 us  [per_device(): pl.pallas_call(functools.partial(kernel, (shards, sections, mps, spans, p...]
where the time goes in v2:
time: 53.4 us; the launch traced here: 53.2 us
  Pallas kernels  51.7 us (97%)
  local copies, waits for them, and re-layouts  1.57 us (3%)
    pallas_call x1, Pallas kernels, per_device(): pl.pallas_call(functools.partial(kernel, (shards, sections, mps, spans, p...  51.7 us
    unnamed x1, local copies, waits for them, and re-layouts  1.57 us

profile of v2, /device:TPU:1, one launch (start us, length us, event | category | flops | bytes accessed | tf_op | source)
XLA Modules:
  0.0 53.2 jit_solution(5742002467100109684)
XLA Ops:
  0.0 51.7 %shard_map.82 = bf16[128,512]{1,0:T(8,128)(2,1)} custom-call(s32[2]{0:T(128)} %slot_span_hbm.1, s32[2]{0:T(128)} %counts_hbm.1, s32[2,256]{1,0:T(2,128)} %ids_hbm.1, bf16[128,512]{1,0:T(8,128)(2,1)} %states_hbm.1, bf16[128,512]{1,0:T(8,128)(2,1)} %queries_hbm.1, bf16[1000,896]{1,0:T(8,128)(2,1)} %table_hbm.1, bf16[512,896]{1,0:T(8,128)(2,1)} %cond_weight_hbm.1, ...), custom_call_target="tpu_custom_call" | custom-call | tf_op jit(solution)/shard_map/pallas_call | solution.py:430
  51.7 1.6 %copy.11 = bf16[128,512]{1,0:T(8,128)(2,1)} copy(bf16[128,512]{1,0:T(8,128)(2,1)} %shard_map.82) | data formatting | bytes 262144

commit v3 on v2

v3 whole, which is shorter than its diff:
```python
import functools
import math

import jax
import jax.numpy as jnp
from jax import lax
from jax.experimental import pallas as pl
from jax.experimental.pallas import tpu as pltpu
from jax.sharding import PartitionSpec as P

HD = 128
LANES = 128
TILE = 16
RINGS = 4
BF16 = jnp.bfloat16
F32 = jnp.float32
MESH = pl.DeviceIdType.MESH


def to_column(row, rows):
    shape = (rows, row.shape[1])
    here = lax.broadcasted_iota(jnp.int32, shape, 0) == lax.broadcasted_iota(jnp.int32, shape, 1)
    return jnp.sum(jnp.where(here, row, 0.0), axis=1, keepdims=True)


def lane_sum(mask, values):
    return jnp.sum(jnp.where(mask, values, 0.0), axis=1, keepdims=True)


def kernel(
    sizes,
    slot_span_hbm,
    counts_hbm,
    ids_hbm,
    states_hbm,
    queries_hbm,
    table_hbm,
    cond_weight_hbm,
    kv_hbm,
    out,
    slot_span,
    counts,
    ids,
    states,
    queries,
    queries_other,
    table,
    cond_weight,
    kv_raw,
    kv_weight,
    kv_other,
    kv_f32,
    facts,
    asked_f32,
    answers,
    arrived,
    picks,
    partial,
    partial_out,
    partial_in,
    condition,
    encoded,
    reply,
    given,
    local_sems,
    facts_sems,
    row_sems,
    part_sems,
    cond_sems,
    enc_send,
    enc_recv,
    pair_send,
    pair_recv,
):
    shards, sections, mps, spans, part, span_len = sizes
    groups = sections * mps
    enc_width = table.shape[1]
    heads = enc_width // LANES
    vocab = table.shape[0]
    me = lax.axis_index("seq")
    section = lax.axis_index("section")
    mp = lax.axis_index("mp")
    group = section * mps + mp
    positions = sections * part

    loads = [
        pltpu.make_async_copy(src, dst, local_sems.at[n])
        for n, (src, dst) in enumerate(
            (
                (states_hbm, states),
                (cond_weight_hbm, cond_weight),
                (table_hbm, table),
                (kv_hbm, kv_raw),
                (queries_hbm, queries),
                (ids_hbm, ids),
                (slot_span_hbm, slot_span),
                (counts_hbm, counts),
            )
        )
    ]
    for n in (5, 6, 7, 3, 0, 1, 2, 4):
        loads[n].start()

    half = shards // 2
    rings = facts.shape[0]

    def seq_peer(d):
        return {"seq": lax.rem(me + d, shards)}

    def over_peers(low, high, act):
        def body(i, carry):
            act(half + (i + 1) // 2 * (1 - 2 * lax.rem(i, 2)))
            return carry

        lax.fori_loop(low, high, body, 0)

    def within(distance):
        return max(0, shards - 1 - 2 * distance)

    reach = [half * (c + 1) // rings for c in range(rings)]
    row_ends = [within(b) for b in [0] + reach]
    fact_ends = [shards - 1] + [within(b + 1) for b in reach]

    def wait_in(ref, sem):
        pltpu.make_async_remote_copy(
            src_ref=ref, dst_ref=ref, send_sem=sem, recv_sem=sem, device_id=seq_peer(1), device_id_type=MESH
        ).wait_recv()

    def wait_out(ref, sem):
        pltpu.make_async_remote_copy(
            src_ref=ref, dst_ref=ref, send_sem=sem, recv_sem=sem, device_id=seq_peer(1), device_id_type=MESH
        ).wait_send()

    def group_peer(ds, dx):
        return {"section": lax.rem(section + ds, sections), "mp": lax.rem(mp + dx, mps)}

    group_steps = [(ds, dx) for ds in range(sections) for dx in range(mps)][1:]

    barrier = pltpu.get_barrier_semaphore()
    facts[...] = jnp.full(facts.shape, -1, jnp.int32)
    over_peers(
        0, shards - 1, lambda d: pl.semaphore_signal(barrier, inc=1, device_id=seq_peer(d), device_id_type=MESH)
    )
    for ds, dx in group_steps:
        pl.semaphore_signal(barrier, inc=1, device_id=group_peer(ds, dx), device_id_type=MESH)

    lane = lax.broadcasted_iota(jnp.int32, (1, LANES), 1)
    for load in loads[5:]:
        load.wait()
    all_ids = ids[...]
    message = jnp.zeros((spans, LANES), jnp.int32)
    lanes_2 = lax.broadcasted_iota(jnp.int32, message.shape, 1)
    for g in range(sections):
        first = g * mps * part // LANES * LANES
        line = pltpu.roll(all_ids[:, first : first + LANES], lax.rem(2 * LANES + g * part - mp * part, LANES), 1)
        message = jnp.where((lanes_2 >= g * part) & (lanes_2 < (g + 1) * part), line, message)
    for k in range(spans):
        here = lax.broadcasted_iota(jnp.int32, message.shape, 0) == k
        message = jnp.where(here & (lanes_2 == positions), slot_span[k], message)
        message = jnp.where(here & (lanes_2 == positions + 1), counts[k], message)
    facts[0, 0:spans, :] = message

    loads[0].wait()
    loads[1].wait()
    product = jnp.dot(states[...], cond_weight[...], preferred_element_type=F32)
    block_rows = product.shape[0] // groups
    partial[...] = product.reshape(groups, block_rows, enc_width)
    partial_out[...] = product.astype(BF16).reshape(groups, block_rows, enc_width)

    loads[3].wait()
    pairs = kv_weight.shape[1] // LANES
    step_rows = kv_f32.shape[0] // pairs

    def split_pairs(step, carry):
        rows = pl.ds(pl.multiple_of(step * step_rows * pairs, TILE), step_rows * pairs)
        kv_f32[...] = kv_raw[rows, :].astype(F32)
        for t in range(pairs // 2):
            for j in range(2):
                column = (j * (pairs // 2) + t) * LANES
                kv_weight[pl.ds(pl.multiple_of(step * step_rows, TILE), step_rows), column : column + LANES] = (
                    kv_f32[pl.ds(t * 2 + j, step_rows, stride=pairs), :].astype(BF16)
                )
        return carry

    lax.fori_loop(0, kv_weight.shape[0] // step_rows, split_pairs, 0)
    asked_f32[...] = jnp.zeros_like(asked_f32)

    pl.semaphore_wait(barrier, shards - 1 + len(group_steps))

    def tell(ring):
        def act(d):
            pltpu.make_async_remote_copy(
                src_ref=facts.at[0, pl.ds(0, spans)],
                dst_ref=facts.at[ring, pl.ds((shards - d) * spans, spans)],
                send_sem=facts_sems.at[rings],
                recv_sem=facts_sems.at[ring],
                device_id=seq_peer(d),
                device_id_type=MESH,
            ).start()

        return act

    for ring in reversed(range(rings)):
        over_peers(fact_ends[ring + 1], fact_ends[ring], tell(ring))

    for ds, dx in group_steps:
        to = lax.rem(section + ds, sections) * mps + lax.rem(mp + dx, mps)
        back = ((sections - ds) % sections) * mps + (mps - dx) % mps
        pltpu.make_async_remote_copy(
            src_ref=partial_out.at[to],
            dst_ref=partial_in.at[back],
            send_sem=part_sems.at[0],
            recv_sem=part_sems.at[1],
            device_id=group_peer(ds, dx),
            device_id_type=MESH,
        ).start()

    def pair_copy(index, src, dst):
        copy = pltpu.make_async_remote_copy(
            src_ref=src,
            dst_ref=dst,
            send_sem=pair_send.at[index],
            recv_sem=pair_recv.at[index],
            device_id=group_peer(1, 0),
            device_id_type=MESH,
        )
        copy.start()
        return copy

    loads[4].wait()
    own_rows = pl.ds(pl.multiple_of(section * span_len, TILE), span_len)
    other_rows = pl.ds(pl.multiple_of((1 - section) * span_len, TILE), span_len)
    pair_copies = [
        pair_copy(0, queries.at[other_rows], queries_other),
        pair_copy(1, kv_weight, kv_other),
    ]

    wide = (shards, LANES)
    lanes = lax.broadcasted_iota(jnp.int32, wide, 1)
    rows_d = lax.broadcasted_iota(jnp.int32, wide, 0)
    span_row = (lax.rem(me + lax.rem(lane, shards), shards) * spans + lane // shards).astype(F32)
    span_row = jnp.where(lane < spans * shards, span_row, -2.0)
    vocab_lane = lax.broadcasted_iota(jnp.int32, (shards, vocab), 1).astype(F32)

    def look_up(told, ring):
        slots = jnp.where(section == 0, told[0], told[1]).astype(F32)
        slot_holds = lane_sum(lanes == positions, slots)
        wanted = span_row == slot_holds
        marks = []
        for g in range(sections):
            want_row = jnp.zeros((1, LANES), F32)
            for k in range(spans):
                local = told[k] - me * vocab
                inside = (local >= 0) & (local < vocab)
                want = lane_sum(inside & (lanes >= g * part) & (lanes < (g + 1) * part), (local + 1).astype(F32))
                want_row += jnp.sum(jnp.where(lanes == rows_d + k * shards, want, 0.0), axis=0, keepdims=True)
            request = lane_sum(wanted, want_row) - 1.0
            marks.append((vocab_lane == request).astype(F32).astype(BF16))
        rows_out = jnp.dot(jnp.concatenate(marks, axis=0), table[...], preferred_element_type=F32)
        for g in range(sections):
            for h in range(heads):
                asked_f32[pl.ds(g * heads + h, shards, stride=TILE), :] = rows_out[
                    g * shards : (g + 1) * shards, h * LANES : (h + 1) * LANES
                ]
        answers[ring] = asked_f32[...].astype(BF16).reshape(answers.shape[1:])

    def answer(ring):
        def act(d):
            pltpu.make_async_remote_copy(
                src_ref=answers.at[ring, d],
                dst_ref=arrived.at[shards - d],
                send_sem=row_sems.at[0],
                recv_sem=row_sems.at[1],
                device_id=seq_peer(d),
                device_id_type=MESH,
            ).start()

        return act

    def sum_condition():
        wait_in(partial_in.at[pl.ds(1, groups - 1)], part_sems.at[1])
        total = partial[group]
        for n in range(1, groups):
            total += partial_in[n].astype(F32)
        condition[mp] = total.astype(BF16)
        for dx in range(1, mps):
            pltpu.make_async_remote_copy(
                src_ref=condition.at[mp],
                dst_ref=condition.at[mp],
                send_sem=cond_sems.at[0],
                recv_sem=cond_sems.at[1],
                device_id=group_peer(0, dx),
                device_id_type=MESH,
            ).start()

    loads[2].wait()
    told = [jnp.full(wide, -1, jnp.int32)] * spans
    for ring in range(rings):
        heard = (fact_ends[ring] - fact_ends[ring + 1]) * spans
        wait_in(facts.at[ring, pl.ds(0, heard)], facts_sems.at[ring])
        told = [jnp.maximum(told[k], facts[ring, pl.ds(k, shards, stride=spans), :]) for k in range(spans)]
        if ring == 0:
            near = told
        look_up(told, ring)
        over_peers(row_ends[ring + 1], row_ends[ring], answer(ring))
        if ring == 0:
            arrived[0] = answers[0, 0]
            sum_condition()

    held = slot_span[section]
    span_at = lax.rem(me + rows_d[:, :1], shards) * spans
    chosen = jnp.zeros((1, LANES), F32)
    for home in range(spans):
        chosen += jnp.sum(jnp.where(span_at + home == held, near[home].astype(F32), 0.0), axis=0, keepdims=True)
    count = lane_sum(lane == positions + 1, chosen)
    owner = jnp.floor((chosen + 0.5) * (1.0 / vocab))
    step = owner - me.astype(F32)
    step = jnp.where(step < 0, step + shards, step)
    column = to_column(step * TILE, positions)
    column += (lax.broadcasted_iota(jnp.int32, column.shape, 0) // part * heads).astype(F32)
    place_lane = lax.broadcasted_iota(jnp.int32, (positions, shards * TILE), 1).astype(F32)
    for h in range(heads):
        picks[h * positions : (h + 1) * positions, :] = (place_lane == column + h).astype(F32).astype(BF16)

    wait_in(condition.at[pl.ds(0, mps - 1)], cond_sems.at[1])
    wait_in(arrived.at[pl.ds(1, shards - 1)], row_sems.at[1])

    embedded = jnp.dot(
        picks[...], arrived[...].reshape(shards * TILE, LANES), preferred_element_type=F32
    )
    embedded_bf16 = embedded.astype(BF16)
    cond = condition[...].reshape(span_len, enc_width)
    scores = []
    for h in range(heads):
        scores.append(
            lax.dot_general(
                embedded_bf16[h * positions : (h + 1) * positions],
                cond[:, h * LANES : (h + 1) * LANES],
                (((1,), (1,)), ((), ())),
                preferred_element_type=F32,
            )
        )
    weights = softmax(jnp.concatenate(scores, axis=0) * (1.0 / math.sqrt(LANES)))
    for h in range(heads):
        added = jnp.dot(
            weights[h * positions : (h + 1) * positions],
            cond[:, h * LANES : (h + 1) * LANES],
            preferred_element_type=F32,
        )
        rows = (embedded[h * positions : (h + 1) * positions] + added).astype(BF16)
        encoded[mp, :, :, h * LANES : (h + 1) * LANES] = rows.reshape(sections, part, LANES)

    over_x = []
    for g in range(sections):
        over_x.append([])
        for dx in range(1, mps):
            copy = pltpu.make_async_remote_copy(
                src_ref=encoded.at[mp, g],
                dst_ref=encoded.at[mp, g],
                send_sem=enc_send.at[g, dx],
                recv_sem=enc_recv.at[g, dx],
                device_id=group_peer(0, dx),
                device_id_type=MESH,
            )
            copy.start()
            over_x[g].append(copy)

    width = kv_weight.shape[1] // 2
    local_heads = width // HD
    row_count = mps * part

    def project(g, weight):
        rows = encoded[:, g].reshape(row_count, enc_width)
        return jnp.dot(rows, weight[...], preferred_element_type=F32).astype(BF16)

    def attend(query, key_value):
        scores = []
        for t in range(local_heads):
            scores.append(
                jnp.concatenate(
                    [
                        lax.dot_general(
                            query[:, t * HD : (t + 1) * HD],
                            block[:, t * HD : (t + 1) * HD],
                            (((1,), (1,)), ((), ())),
                            preferred_element_type=F32,
                        )
                        for block in key_value
                    ],
                    axis=1,
                )
            )
        scores = jnp.concatenate(scores, axis=0) * (1.0 / math.sqrt(HD))
        neighbour = lax.broadcasted_iota(jnp.int32, scores.shape, 1) // row_count
        weights = softmax(jnp.where(neighbour.astype(F32) < count, scores, -jnp.inf))
        done = []
        for t in range(local_heads):
            added = [
                jnp.dot(
                    weights[t * span_len : (t + 1) * span_len, n * row_count : (n + 1) * row_count],
                    block[:, width + t * HD : width + (t + 1) * HD],
                    preferred_element_type=F32,
                )
                for n, block in enumerate(key_value)
            ]
            done.append(functools.reduce(jnp.add, added).astype(BF16))
        return jnp.concatenate(done, axis=1)

    for copy in pair_copies:
        copy.wait_recv()
    theirs, ours = [], []
    for g in range(sections):
        for copy in over_x[g]:
            copy.wait_recv()
        theirs.append(project(g, kv_other))
        if g + 1 < sections:
            ours.append(project(g, kv_weight))
    reply[...] = attend(queries_other[...], theirs)
    pair_copies.append(pair_copy(2, reply, given))
    ours.append(project(sections - 1, kv_weight))
    out[own_rows, :] = attend(queries[own_rows, :], ours)

    wait_out(facts.at[0, pl.ds(0, (shards - 1) * spans)], facts_sems.at[rings])
    wait_out(answers.at[0, pl.ds(1, shards - 1)], row_sems.at[0])
    wait_out(partial_out.at[pl.ds(1, groups - 1)], part_sems.at[0])
    wait_out(condition.at[pl.ds(1, mps - 1)], cond_sems.at[0])
    for copy in sum(over_x, []) + pair_copies:
        copy.wait_send()
    pair_copies[-1].wait_recv()
    out[other_rows, :] = given[...]


def softmax(scores):
    high = jnp.max(scores, axis=1, keepdims=True)
    raised = jnp.exp(scores - high)
    return (raised / jnp.sum(raised, axis=1, keepdims=True)).astype(BF16)


def per_device(
    mesh_shape, span_states, queries, slot_span, neighbour_ids, neighbour_count, table, cond_weight, kv_weight
):
    shards, sections, mps = mesh_shape["seq"], mesh_shape["section"], mesh_shape["mp"]
    groups = sections * mps
    spans = slot_span.shape[0]
    part = neighbour_ids.shape[1] // groups
    tokens, width = queries.shape
    vocab, enc_width = table.shape
    pairs = 2 * width // LANES
    kv_rows = (
        kv_weight.reshape(enc_width, 2, width // LANES, LANES)
        .transpose(0, 2, 1, 3)
        .reshape(enc_width * pairs, LANES)
    )
    vmem = pl.BlockSpec(memory_space=pltpu.VMEM)
    hbm = pl.BlockSpec(memory_space=pltpu.HBM)
    rows_out = groups // mps * (enc_width // LANES)
    block_rows = tokens // groups
    span_len = tokens // spans
    dma = pltpu.SemaphoreType.DMA
    return pl.pallas_call(
        functools.partial(kernel, (shards, sections, mps, spans, part, span_len)),
        out_shape=jax.ShapeDtypeStruct(queries.shape, queries.dtype),
        in_specs=[hbm] * 8,
        out_specs=vmem,
        scratch_shapes=[
            pltpu.SMEM(slot_span.shape, jnp.int32),
            pltpu.SMEM(neighbour_count.shape, jnp.int32),
            pltpu.VMEM(neighbour_ids.shape, jnp.int32),
            pltpu.VMEM(span_states.shape, BF16),
            pltpu.VMEM(queries.shape, BF16),
            pltpu.VMEM((span_len, width), BF16),
            pltpu.VMEM(table.shape, BF16),
            pltpu.VMEM(cond_weight.shape, BF16),
            pltpu.VMEM(kv_rows.shape, BF16),
            pltpu.VMEM((enc_width, 2 * width), BF16),
            pltpu.VMEM((enc_width, 2 * width), BF16),
            pltpu.VMEM((enc_width // 8 * pairs, LANES), F32),
            pltpu.VMEM((RINGS, shards * spans, LANES), jnp.int32),
            pltpu.VMEM((shards * TILE, LANES), F32),
            pltpu.VMEM((RINGS, shards, TILE, LANES), BF16),
            pltpu.VMEM((shards, TILE, LANES), BF16),
            pltpu.VMEM((rows_out * part, shards * TILE), BF16),
            pltpu.VMEM((groups, block_rows, enc_width), F32),
            pltpu.VMEM((groups, block_rows, enc_width), BF16),
            pltpu.VMEM((groups, block_rows, enc_width), BF16),
            pltpu.VMEM((mps, block_rows, enc_width), BF16),
            pltpu.VMEM((mps, sections, part, enc_width), BF16),
            pltpu.VMEM((span_len, width), BF16),
            pltpu.VMEM((span_len, width), BF16),
            dma((8,)),
            dma((RINGS + 1,)),
            dma((2,)),
            dma((2,)),
            dma((2,)),
            dma((sections, mps)),
            dma((sections, mps)),
            dma((3,)),
            dma((3,)),
        ],
        compiler_params=pltpu.CompilerParams(
            collective_id=0, has_side_effects=True, vmem_limit_bytes=60 * 1024 * 1024
        ),
    )(slot_span, neighbour_count, neighbour_ids, span_states, queries, table, cond_weight, kv_rows)


def solution(mesh):
    placed = (
        P("seq", ("section", "mp")),
        P("seq", ("section", "mp")),
        P("seq"),
        P("seq", None),
        P("seq"),
        P("seq", None),
        P(("section", "mp"), None),
        P(None, None, ("section", "mp")),
    )
    return jax.shard_map(
        functools.partial(per_device, dict(mesh.shape)),
        mesh=mesh,
        in_specs=placed,
        out_specs=P("seq", ("section", "mp")),
        check_vma=False,
    )
```

time: 53.4 us -> 52.3 us (0.979)
  Pallas kernels: 51.7 us -> 50.6 us
    pallas_call x1, Pallas kernels: 51.7 us -> 50.6 us  [per_device(): pl.pallas_call(functools.partial(kernel, (shards, sections, mps, spans, p...]
where the time goes in v3:
time: 52.3 us; the launch traced here: 52.2 us
  Pallas kernels  50.6 us (97%)
  local copies, waits for them, and re-layouts  1.57 us (3%)
    pallas_call x1, Pallas kernels, per_device(): pl.pallas_call(functools.partial(kernel, (shards, sections, mps, spans, p...  50.6 us
    unnamed x1, local copies, waits for them, and re-layouts  1.57 us

profile of v3, /device:TPU:1, one launch (start us, length us, event | category | flops | bytes accessed | tf_op | source)
XLA Modules:
  0.0 52.2 jit_solution(6791165906322408602)
XLA Ops:
  0.0 50.6 %shard_map.82 = bf16[128,512]{1,0:T(8,128)(2,1)} custom-call(s32[2]{0:T(128)} %slot_span_hbm.1, s32[2]{0:T(128)} %counts_hbm.1, s32[2,256]{1,0:T(2,128)} %ids_hbm.1, bf16[128,512]{1,0:T(8,128)(2,1)} %states_hbm.1, bf16[128,512]{1,0:T(8,128)(2,1)} %queries_hbm.1, bf16[1000,896]{1,0:T(8,128)(2,1)} %table_hbm.1, bf16[512,896]{1,0:T(8,128)(2,1)} %cond_weight_hbm.1, ...), custom_call_target="tpu_custom_call" | custom-call | tf_op jit(solution)/shard_map/pallas_call | solution.py:460
  50.6 1.6 %copy.11 = bf16[128,512]{1,0:T(8,128)(2,1)} copy(bf16[128,512]{1,0:T(8,128)(2,1)} %shard_map.82) | data formatting | bytes 262144

commit v4 on v3

--- a/solution.py
+++ b/solution.py
@@ -11,7 +11,7 @@
 HD = 128
 LANES = 128
 TILE = 16
-RINGS = 4
+RINGS = 2
 BF16 = jnp.bfloat16
 F32 = jnp.float32
 MESH = pl.DeviceIdType.MESH
@@ -98,9 +98,6 @@
             )
         )
     ]
-    for n in (5, 6, 7, 3, 0, 1, 2, 4):
-        loads[n].start()
-
     half = shards // 2
     rings = facts.shape[0]
 
@@ -114,12 +111,10 @@
 
         lax.fori_loop(low, high, body, 0)
 
-    def within(distance):
-        return max(0, shards - 1 - 2 * distance)
-
-    reach = [half * (c + 1) // rings for c in range(rings)]
-    row_ends = [within(b) for b in [0] + reach]
-    fact_ends = [shards - 1] + [within(b + 1) for b in reach]
+    ring_width = shards // rings
+    fact_counts = [ring_width + 2] + [ring_width] * (rings - 2) + [ring_width - 2] if rings > 1 else [shards]
+    fact_ring = jnp.where(me == shards - 1, 0, jnp.maximum(me - 1, 0) // ring_width)
+    own_facts = pl.ds(me * spans, spans)
 
     def wait_in(ref, sem):
         pltpu.make_async_remote_copy(
@@ -143,6 +138,9 @@
     )
     for ds, dx in group_steps:
         pl.semaphore_signal(barrier, inc=1, device_id=group_peer(ds, dx), device_id_type=MESH)
+
+    for n in (5, 6, 7, 3, 0, 1, 2, 4):
+        loads[n].start()
 
     lane = lax.broadcasted_iota(jnp.int32, (1, LANES), 1)
     for load in loads[5:]:
@@ -158,7 +156,7 @@
         here = lax.broadcasted_iota(jnp.int32, message.shape, 0) == k
         message = jnp.where(here & (lanes_2 == positions), slot_span[k], message)
         message = jnp.where(here & (lanes_2 == positions + 1), counts[k], message)
-    facts[0, 0:spans, :] = message
+    facts[fact_ring, own_facts, :] = message
 
     loads[0].wait()
     loads[1].wait()
@@ -187,21 +185,17 @@
 
     pl.semaphore_wait(barrier, shards - 1 + len(group_steps))
 
-    def tell(ring):
-        def act(d):
-            pltpu.make_async_remote_copy(
-                src_ref=facts.at[0, pl.ds(0, spans)],
-                dst_ref=facts.at[ring, pl.ds((shards - d) * spans, spans)],
-                send_sem=facts_sems.at[rings],
-                recv_sem=facts_sems.at[ring],
-                device_id=seq_peer(d),
-                device_id_type=MESH,
-            ).start()
-
-        return act
-
-    for ring in reversed(range(rings)):
-        over_peers(fact_ends[ring + 1], fact_ends[ring], tell(ring))
+    def tell(d):
+        pltpu.make_async_remote_copy(
+            src_ref=facts.at[fact_ring, own_facts],
+            dst_ref=facts.at[fact_ring, own_facts],
+            send_sem=facts_sems.at[rings],
+            recv_sem=facts_sems.at[fact_ring],
+            device_id=seq_peer(d),
+            device_id_type=MESH,
+        ).start()
+
+    over_peers(0, shards - 1, tell)
 
     for ds, dx in group_steps:
         to = lax.rem(section + ds, sections) * mps + lax.rem(mp + dx, mps)
@@ -237,15 +231,15 @@
 
     wide = (shards, LANES)
     lanes = lax.broadcasted_iota(jnp.int32, wide, 1)
-    rows_d = lax.broadcasted_iota(jnp.int32, wide, 0)
-    span_row = (lax.rem(me + lax.rem(lane, shards), shards) * spans + lane // shards).astype(F32)
+    rows_j = lax.broadcasted_iota(jnp.int32, wide, 0)
+    span_row = (lax.rem(lane, shards) * spans + lane // shards).astype(F32)
     span_row = jnp.where(lane < spans * shards, span_row, -2.0)
-    vocab_lane = lax.broadcasted_iota(jnp.int32, (shards, vocab), 1).astype(F32)
+    vocab_lane = lax.broadcasted_iota(jnp.int32, (ring_width, vocab), 1).astype(F32)
 
     def look_up(told, ring):
         slots = jnp.where(section == 0, told[0], told[1]).astype(F32)
-        slot_holds = lane_sum(lanes == positions, slots)
-        wanted = span_row == slot_holds
+        slots = slots[ring * ring_width : (ring + 1) * ring_width]
+        wanted = span_row == lane_sum(lanes[:ring_width] == positions, slots)
         marks = []
         for g in range(sections):
             want_row = jnp.zeros((1, LANES), F32)
@@ -253,29 +247,35 @@
                 local = told[k] - me * vocab
                 inside = (local >= 0) & (local < vocab)
                 want = lane_sum(inside & (lanes >= g * part) & (lanes < (g + 1) * part), (local + 1).astype(F32))
-                want_row += jnp.sum(jnp.where(lanes == rows_d + k * shards, want, 0.0), axis=0, keepdims=True)
+                want_row += jnp.sum(jnp.where(lanes == rows_j + k * shards, want, 0.0), axis=0, keepdims=True)
             request = lane_sum(wanted, want_row) - 1.0
             marks.append((vocab_lane == request).astype(F32).astype(BF16))
         rows_out = jnp.dot(jnp.concatenate(marks, axis=0), table[...], preferred_element_type=F32)
         for g in range(sections):
             for h in range(heads):
-                asked_f32[pl.ds(g * heads + h, shards, stride=TILE), :] = rows_out[
-                    g * shards : (g + 1) * shards, h * LANES : (h + 1) * LANES
+                asked_f32[pl.ds(g * heads + h, ring_width, stride=TILE), :] = rows_out[
+                    g * ring_width : (g + 1) * ring_width, h * LANES : (h + 1) * LANES
                 ]
         answers[ring] = asked_f32[...].astype(BF16).reshape(answers.shape[1:])
 
     def answer(ring):
-        def act(d):
-            pltpu.make_async_remote_copy(
-                src_ref=answers.at[ring, d],
-                dst_ref=arrived.at[shards - d],
-                send_sem=row_sems.at[0],
-                recv_sem=row_sems.at[1],
-                device_id=seq_peer(d),
-                device_id_type=MESH,
-            ).start()
-
-        return act
+        def act(n, carry):
+            to = ring * ring_width + n
+
+            @pl.when(to != me)
+            def _():
+                pltpu.make_async_remote_copy(
+                    src_ref=answers.at[ring, n],
+                    dst_ref=arrived.at[me],
+                    send_sem=row_sems.at[0],
+                    recv_sem=row_sems.at[1],
+                    device_id={"seq": to},
+                    device_id_type=MESH,
+                ).start()
+
+            return carry
+
+        lax.fori_loop(0, ring_width, act, 0)
 
     def sum_condition():
         wait_in(partial_in.at[pl.ds(1, groups - 1)], part_sems.at[1])
@@ -296,27 +296,31 @@
     loads[2].wait()
     told = [jnp.full(wide, -1, jnp.int32)] * spans
     for ring in range(rings):
-        heard = (fact_ends[ring] - fact_ends[ring + 1]) * spans
-        wait_in(facts.at[ring, pl.ds(0, heard)], facts_sems.at[ring])
+        heard = facts.at[ring, pl.ds(0, fact_counts[ring] * spans)]
+        heard_others = facts.at[ring, pl.ds(0, (fact_counts[ring] - 1) * spans)]
+
+        @pl.when(fact_ring == ring)
+        def _():
+            wait_in(heard_others, facts_sems.at[ring])
+
+        @pl.when(fact_ring != ring)
+        def _():
+            wait_in(heard, facts_sems.at[ring])
+
         told = [jnp.maximum(told[k], facts[ring, pl.ds(k, shards, stride=spans), :]) for k in range(spans)]
-        if ring == 0:
-            near = told
         look_up(told, ring)
-        over_peers(row_ends[ring + 1], row_ends[ring], answer(ring))
-        if ring == 0:
-            arrived[0] = answers[0, 0]
-            sum_condition()
+        answer(ring)
+    arrived[me] = answers[me // ring_width, lax.rem(me, ring_width)]
+    sum_condition()
 
     held = slot_span[section]
-    span_at = lax.rem(me + rows_d[:, :1], shards) * spans
+    span_at = rows_j[:, :1] * spans
     chosen = jnp.zeros((1, LANES), F32)
     for home in range(spans):
-        chosen += jnp.sum(jnp.where(span_at + home == held, near[home].astype(F32), 0.0), axis=0, keepdims=True)
+        chosen += jnp.sum(jnp.where(span_at + home == held, told[home].astype(F32), 0.0), axis=0, keepdims=True)
     count = lane_sum(lane == positions + 1, chosen)
     owner = jnp.floor((chosen + 0.5) * (1.0 / vocab))
-    step = owner - me.astype(F32)
-    step = jnp.where(step < 0, step + shards, step)
-    column = to_column(step * TILE, positions)
+    column = to_column(owner * TILE, positions)
     column += (lax.broadcasted_iota(jnp.int32, column.shape, 0) // part * heads).astype(F32)
     place_lane = lax.broadcasted_iota(jnp.int32, (positions, shards * TILE), 1).astype(F32)
     for h in range(heads):
@@ -421,7 +425,7 @@
     out[own_rows, :] = attend(queries[own_rows, :], ours)
 
     wait_out(facts.at[0, pl.ds(0, (shards - 1) * spans)], facts_sems.at[rings])
-    wait_out(answers.at[0, pl.ds(1, shards - 1)], row_sems.at[0])
+    wait_out(arrived.at[pl.ds(1, shards - 1)], row_sems.at[0])
     wait_out(partial_out.at[pl.ds(1, groups - 1)], part_sems.at[0])
     wait_out(condition.at[pl.ds(1, mps - 1)], cond_sems.at[0])
     for copy in sum(over_x, []) + pair_copies:
@@ -476,8 +480,8 @@
             pltpu.VMEM((enc_width, 2 * width), BF16),
             pltpu.VMEM((enc_width // 8 * pairs, LANES), F32),
             pltpu.VMEM((RINGS, shards * spans, LANES), jnp.int32),
-            pltpu.VMEM((shards * TILE, LANES), F32),
-            pltpu.VMEM((RINGS, shards, TILE, LANES), BF16),
+            pltpu.VMEM((shards // RINGS * TILE, LANES), F32),
+            pltpu.VMEM((RINGS, shards // RINGS, TILE, LANES), BF16),
             pltpu.VMEM((shards, TILE, LANES), BF16),
             pltpu.VMEM((rows_out * part, shards * TILE), BF16),
             pltpu.VMEM((groups, block_rows, enc_width), F32),

time: 52.3 us -> 49.5 us (0.946); the launches traced: 52.2 us -> 48.8 us
  Pallas kernels: 50.6 us -> 47.2 us
    pallas_call x1, Pallas kernels: 50.6 us -> 47.2 us  [per_device(): pl.pallas_call(functools.partial(kernel, (shards, sections, mps, spans, p...]
where the time goes in v4:
time: 49.5 us; the launch traced here: 48.8 us
  Pallas kernels  47.2 us (95%)
  local copies, waits for them, and re-layouts  1.57 us (3%)
    pallas_call x1, Pallas kernels, per_device(): pl.pallas_call(functools.partial(kernel, (shards, sections, mps, spans, p...  47.2 us
    unnamed x1, local copies, waits for them, and re-layouts  1.57 us

profile of v4, /device:TPU:1, one launch (start us, length us, event | category | flops | bytes accessed | tf_op | source)
XLA Modules:
  0.0 48.8 jit_solution(13829068226239064285)
XLA Ops:
  0.0 47.2 %shard_map.82 = bf16[128,512]{1,0:T(8,128)(2,1)} custom-call(s32[2]{0:T(128)} %slot_span_hbm.1, s32[2]{0:T(128)} %counts_hbm.1, s32[2,256]{1,0:T(2,128)} %ids_hbm.1, bf16[128,512]{1,0:T(8,128)(2,1)} %states_hbm.1, bf16[128,512]{1,0:T(8,128)(2,1)} %queries_hbm.1, bf16[1000,896]{1,0:T(8,128)(2,1)} %table_hbm.1, bf16[512,896]{1,0:T(8,128)(2,1)} %cond_weight_hbm.1, ...), custom_call_target="tpu_custom_call" | custom-call | tf_op jit(solution)/shard_map/pallas_call | solution.py:464
  47.2 1.6 %copy.11 = bf16[128,512]{1,0:T(8,128)(2,1)} copy(bf16[128,512]{1,0:T(8,128)(2,1)} %shard_map.82) | data formatting | bytes 262144

commit v5 on v4

--- a/solution.py
+++ b/solution.py
@@ -11,7 +11,7 @@
 HD = 128
 LANES = 128
 TILE = 16
-RINGS = 2
+RINGS = 4
 BF16 = jnp.bfloat16
 F32 = jnp.float32
 MESH = pl.DeviceIdType.MESH
@@ -29,18 +29,13 @@
 
 def kernel(
     sizes,
-    slot_span_hbm,
-    counts_hbm,
-    ids_hbm,
+    own_info,
     states_hbm,
     queries_hbm,
     table_hbm,
     cond_weight_hbm,
     kv_hbm,
     out,
-    slot_span,
-    counts,
-    ids,
     states,
     queries,
     queries_other,
@@ -92,9 +87,6 @@
                 (table_hbm, table),
                 (kv_hbm, kv_raw),
                 (queries_hbm, queries),
-                (ids_hbm, ids),
-                (slot_span_hbm, slot_span),
-                (counts_hbm, counts),
             )
         )
     ]
@@ -139,13 +131,12 @@
     for ds, dx in group_steps:
         pl.semaphore_signal(barrier, inc=1, device_id=group_peer(ds, dx), device_id_type=MESH)
 
-    for n in (5, 6, 7, 3, 0, 1, 2, 4):
+    for n in (3, 0, 1, 2, 4):
         loads[n].start()
 
     lane = lax.broadcasted_iota(jnp.int32, (1, LANES), 1)
-    for load in loads[5:]:
-        load.wait()
-    all_ids = ids[...]
+    all_ids = own_info[0:spans, :]
+    own_line = own_info[spans : spans + 1, :]
     message = jnp.zeros((spans, LANES), jnp.int32)
     lanes_2 = lax.broadcasted_iota(jnp.int32, message.shape, 1)
     for g in range(sections):
@@ -154,8 +145,8 @@
         message = jnp.where((lanes_2 >= g * part) & (lanes_2 < (g + 1) * part), line, message)
     for k in range(spans):
         here = lax.broadcasted_iota(jnp.int32, message.shape, 0) == k
-        message = jnp.where(here & (lanes_2 == positions), slot_span[k], message)
-        message = jnp.where(here & (lanes_2 == positions + 1), counts[k], message)
+        message = jnp.where(here & (lanes_2 == positions), own_line[:, k : k + 1], message)
+        message = jnp.where(here & (lanes_2 == positions + 1), own_line[:, spans + k : spans + k + 1], message)
     facts[fact_ring, own_facts, :] = message
 
     loads[0].wait()
@@ -313,7 +304,7 @@
     arrived[me] = answers[me // ring_width, lax.rem(me, ring_width)]
     sum_condition()
 
-    held = slot_span[section]
+    held = jnp.where(section == 0, own_line[:, 0:1], own_line[:, 1:2])
     span_at = rows_j[:, :1] * spans
     chosen = jnp.zeros((1, LANES), F32)
     for home in range(spans):
@@ -321,41 +312,45 @@
     count = lane_sum(lane == positions + 1, chosen)
     owner = jnp.floor((chosen + 0.5) * (1.0 / vocab))
     column = to_column(owner * TILE, positions)
-    column += (lax.broadcasted_iota(jnp.int32, column.shape, 0) // part * heads).astype(F32)
-    place_lane = lax.broadcasted_iota(jnp.int32, (positions, shards * TILE), 1).astype(F32)
-    for h in range(heads):
-        picks[h * positions : (h + 1) * positions, :] = (place_lane == column + h).astype(F32).astype(BF16)
+    place_lane = lax.broadcasted_iota(jnp.int32, (part, shards * TILE), 1).astype(F32)
+    for g in range(sections):
+        for h in range(heads):
+            r = g * heads + h
+            picks[r * part : (r + 1) * part, :] = (
+                (place_lane == column[g * part : (g + 1) * part] + r).astype(F32).astype(BF16)
+            )
 
     wait_in(condition.at[pl.ds(0, mps - 1)], cond_sems.at[1])
     wait_in(arrived.at[pl.ds(1, shards - 1)], row_sems.at[1])
 
-    embedded = jnp.dot(
-        picks[...], arrived[...].reshape(shards * TILE, LANES), preferred_element_type=F32
-    )
-    embedded_bf16 = embedded.astype(BF16)
     cond = condition[...].reshape(span_len, enc_width)
-    scores = []
-    for h in range(heads):
-        scores.append(
-            lax.dot_general(
-                embedded_bf16[h * positions : (h + 1) * positions],
+    rows_in = arrived[...].reshape(shards * TILE, LANES)
+    over_x = []
+    for g in range(sections):
+        embedded = jnp.dot(
+            picks[g * heads * part : (g + 1) * heads * part, :], rows_in, preferred_element_type=F32
+        )
+        embedded_bf16 = embedded.astype(BF16)
+        scores = []
+        for h in range(heads):
+            scores.append(
+                lax.dot_general(
+                    embedded_bf16[h * part : (h + 1) * part],
+                    cond[:, h * LANES : (h + 1) * LANES],
+                    (((1,), (1,)), ((), ())),
+                    preferred_element_type=F32,
+                )
+            )
+        weights = softmax(jnp.concatenate(scores, axis=0) * (1.0 / math.sqrt(LANES)))
+        for h in range(heads):
+            added = jnp.dot(
+                weights[h * part : (h + 1) * part],
                 cond[:, h * LANES : (h + 1) * LANES],
-                (((1,), (1,)), ((), ())),
                 preferred_element_type=F32,
             )
-        )
-    weights = softmax(jnp.concatenate(scores, axis=0) * (1.0 / math.sqrt(LANES)))
-    for h in range(heads):
-        added = jnp.dot(
-            weights[h * positions : (h + 1) * positions],
-            cond[:, h * LANES : (h + 1) * LANES],
-            preferred_element_type=F32,
-        )
-        rows = (embedded[h * positions : (h + 1) * positions] + added).astype(BF16)
-        encoded[mp, :, :, h * LANES : (h + 1) * LANES] = rows.reshape(sections, part, LANES)
-
-    over_x = []
-    for g in range(sections):
+            encoded[mp, g, :, h * LANES : (h + 1) * LANES] = (
+                embedded[h * part : (h + 1) * part] + added
+            ).astype(BF16)
         over_x.append([])
         for dx in range(1, mps):
             copy = pltpu.make_async_remote_copy(
@@ -455,6 +450,9 @@
         .transpose(0, 2, 1, 3)
         .reshape(enc_width * pairs, LANES)
     )
+    line = jnp.concatenate([slot_span, neighbour_count])
+    line = jnp.pad(line, (0, neighbour_ids.shape[1] - line.shape[0]))
+    own_info = jnp.concatenate([neighbour_ids, line[None]], axis=0)
     vmem = pl.BlockSpec(memory_space=pltpu.VMEM)
     hbm = pl.BlockSpec(memory_space=pltpu.HBM)
     rows_out = groups // mps * (enc_width // LANES)
@@ -464,12 +462,9 @@
     return pl.pallas_call(
         functools.partial(kernel, (shards, sections, mps, spans, part, span_len)),
         out_shape=jax.ShapeDtypeStruct(queries.shape, queries.dtype),
-        in_specs=[hbm] * 8,
+        in_specs=[vmem] + [hbm] * 5,
         out_specs=vmem,
         scratch_shapes=[
-            pltpu.SMEM(slot_span.shape, jnp.int32),
-            pltpu.SMEM(neighbour_count.shape, jnp.int32),
-            pltpu.VMEM(neighbour_ids.shape, jnp.int32),
             pltpu.VMEM(span_states.shape, BF16),
             pltpu.VMEM(queries.shape, BF16),
             pltpu.VMEM((span_len, width), BF16),
@@ -491,7 +486,7 @@
             pltpu.VMEM((mps, sections, part, enc_width), BF16),
             pltpu.VMEM((span_len, width), BF16),
             pltpu.VMEM((span_len, width), BF16),
-            dma((8,)),
+            dma((5,)),
             dma((RINGS + 1,)),
             dma((2,)),
             dma((2,)),
@@ -502,9 +497,9 @@
             dma((3,)),
         ],
         compiler_params=pltpu.CompilerParams(
-            collective_id=0, has_side_effects=True, vmem_limit_bytes=60 * 1024 * 1024
+            collective_id=0, has_side_effects=True, vmem_limit_bytes=(53 * 1024 + 768) * 1024
         ),
-    )(slot_span, neighbour_count, neighbour_ids, span_states, queries, table, cond_weight, kv_rows)
+    )(own_info, span_states, queries, table, cond_weight, kv_rows)
 
 
 def solution(mesh):

time: 49.5 us -> 49.2 us (level)
  the two profiles are of different devices: /device:TPU:1 before, /device:TPU:449 now
where the time goes in v5:
time: 49.2 us; the launch traced here: 49 us
  Pallas kernels  46.9 us (95%)
  other arithmetic  1.43 us (3%)
  local copies, waits for them, and re-layouts  0.66 us (1%)
    pallas_call x1, Pallas kernels, per_device(): pl.pallas_call(functools.partial(kernel, (shards, sections, mps, spans, p...  46.9 us

profile of v5, /device:TPU:449, one launch (start us, length us, event | category | flops | bytes accessed | tf_op | source)
XLA Modules:
  0.0 49.0 jit_solution(18081571951307436212)
XLA Ops:
  0.0 0.7 %pad_add_fusion.1 = s32[4]{0:T(128)S(1)} fusion(s32[2]{0:T(128)} %param.12, s32[2]{0:T(128)} %param.10), kind=kLoop, calls=%fused_computation.1 | loop fusion | flops 4 | bytes 32 | tf_op jit(solution)/shard_map/concatenate | solution.py:453
  0.8 0.7 %pad_add_fusion.own_info = s32[3,256]{1,0:T(4,128)S(1)} fusion(s32[1,256]{1,0:T(1,128)S(1)} %bitcast.7, s32[2,256]{1,0:T(2,128)} %param.11), kind=kLoop, calls=%fused_computation | loop fusion | flops 768 | bytes 6144 | tf_op jit(solution)/shard_map/concatenate | solution.py:455
  1.4 46.9 %shard_map.82 = bf16[128,512]{1,0:T(8,128)(2,1)S(1)} custom-call(s32[3,256]{1,0:T(4,128)S(1)} %pad_add_fusion.own_info, bf16[128,512]{1,0:T(8,128)(2,1)} %states_hbm.1, bf16[128,512]{1,0:T(8,128)(2,1)} %queries_hbm.1, bf16[1000,896]{1,0:T(8,128)(2,1)} %table_hbm.1, bf16[512,896]{1,0:T(8,128)(2,1)} %cond_weight_hbm.1, bf16[7168,128]{1,0:T(8,128)(2,1)} %bitcast.6), custom_call_target="tpu_custom_call" | custom-call | tf_op jit(solution)/shard_map/pallas_call | solution.py:462
  48.4 0.7 %copy.11 = bf16[128,512]{1,0:T(8,128)(2,1)} copy(bf16[128,512]{1,0:T(8,128)(2,1)S(1)} %shard_map.82) | data formatting | bytes 262144
  (1 shorter events, 0.0 us)
